TPU v7x, 32 devices: a whole 2x2x4 slice. The times are simulated.
32 devices in a mesh: grp: 4 (over x, core), seq: 8 (over z, y).
Axes of the slice: x: 2, y: 2, z: 4, core: 2. Of those that a mesh axis runs over, the one named last changes fastest.
Arguments:
- fields: bfloat16 [8, 2048, 1104], P('grp', 'seq'), may hold values from -6 to 6
- targets: bfloat16 [8, 2048, 1104], P('grp', 'seq'), may hold values from -6 to 6
- land_mask: int32 [8, 2048, 69], P('grp', 'seq'), may hold values from 0 to 1
- interval: int32 [8], P('grp'), may hold values from 0 to 2, as said below
- samples: int32 [8], P('grp'), may hold values from 4 to 13, as said below
- wide_weights: float32 [384, 7632], P('grp')
- wide_firsts: float32 [384, 7632], P('grp'), may hold values from -0.00036621094 to 0.00036621094
- wide_seconds: float32 [384, 7632], P('grp'), may hold values from 6.3374056e-10 to 2.5349622e-09
- tall_weights: float32 [2640, 384], P(None, 'grp')
- tall_firsts: float32 [2640, 384], P(None, 'grp'), may hold values from -0.00036621094 to 0.00036621094
- tall_seconds: float32 [2640, 384], P(None, 'grp'), may hold values from 6.3374056e-10 to 2.5349622e-09
- query_vector: float32 [384], P('grp'), may hold values from -4 to 4
- query_firsts: float32 [384], P('grp'), may hold values from -0.00036621094 to 0.00036621094
- query_seconds: float32 [384], P('grp'), may hold values from 6.3374056e-10 to 2.5349622e-09
Outputs:
- loss_sum: float32 [], replicated
- weight_sum: float32 [], replicated
- grad_norm: float32 [], replicated
- wide_master: float32 [384, 7632], P('grp')
- wide_momentum: float32 [384, 7632], P('grp')
- wide_variance: float32 [384, 7632], P('grp')
- wide_copy: bfloat16 [384, 7632], P('grp')
- tall_master: float32 [2640, 384], P(None, 'grp')
- tall_momentum: float32 [2640, 384], P(None, 'grp')
- tall_variance: float32 [2640, 384], P(None, 'grp')
- tall_copy: bfloat16 [2640, 384], P(None, 'grp')
- query_master: float32 [384], P('grp')
- query_momentum: float32 [384], P('grp')
- query_variance: float32 [384], P('grp')
- query_copy: bfloat16 [384], P('grp')
Inputs may be any that keep to these rules, and one draw needn't show every extreme that they name: `samples`: the first forecast has the smallest count and the last the largest. The lead time is 6 * 2**interval hours; each of the three ids is used by some forecast, and the interval groups are of uneven sizes.
All inputs are finite; a program needn't handle non-finite values.
Results may differ from a plain program's by a relative error of at most 0.023.
Values may be sent and summed in bfloat16 or wider, within the bound.
No kernel may reach another device: no remote copies, remote signals or barrier semaphores. Data moves between devices by JAX's collectives and lax.ppermute only.
A program may use at most 384 MiB of HBM per device.

v0:
```python
import jax
import jax.numpy as jnp
from jax import lax
from jax.sharding import PartitionSpec as P

HEADS = 6
FF = 1536
VARS = 69
PIX = 16
COLS = 128
STEP = 5


beta_first = 0.5
beta_second = 0.5
learn_rate = 0.1
decay_rate = 0.01
adam_epsilon = 1e-08
clip_limit = 0.05
norm_epsilon = 1e-06
masked_score = -1e30


def product(spec, left, right):
    return jnp.einsum(spec, left, right, preferred_element_type=jnp.float32)


def precise(spec, left, right):
    return jnp.einsum(spec, left, right, precision=lax.Precision.HIGHEST)


def layer_norm(values):
    centered = values - jnp.mean(values, axis=-1, keepdims=True)
    return centered * lax.rsqrt(
        jnp.mean(centered * centered, axis=-1, keepdims=True) + norm_epsilon
    )


def modulate(values, shift, scale):
    return layer_norm(values) * (1.0 + scale) + shift


def gelu_tanh(values):
    return jax.nn.gelu(values, approximate=True)


def lead_features(interval, width):
    hours = 6.0 * jnp.exp2(interval.astype(jnp.float32))
    half = width // 2
    freqs = jnp.exp(-jnp.log(1000.0) * jnp.arange(half, dtype=jnp.float32) / half)
    angles = hours[:, None] * freqs[None, :]
    return jax.nn.silu(jnp.concatenate([jnp.sin(angles), jnp.cos(angles)], axis=-1))


def adamw_update(param, first, second, grad):
    first = beta_first * first + (1.0 - beta_first) * grad
    second = beta_second * second + (1.0 - beta_second) * grad * grad
    mean_hat = first / (1.0 - beta_first**STEP)
    var_hat = second / (1.0 - beta_second**STEP)
    param = param - learn_rate * (
        mean_hat / (jnp.sqrt(var_hat) + adam_epsilon) + decay_rate * param
    )
    return (param, first, second, param.astype(jnp.bfloat16))


def block_grads(query_heads, key_heads, value_heads, grad_heads, logsum, delta, scale):
    scores = product("iqhc,inhc->ihqn", query_heads, key_heads) * scale
    probs = jnp.exp(scores - logsum[..., None])
    grad_probs = product("iqhc,inhc->ihqn", grad_heads, value_heads)
    grad_scores = (probs * (grad_probs - delta[..., None])).astype(jnp.bfloat16)
    return (probs.astype(jnp.bfloat16), grad_scores)


def per_device(
    fields,
    targets,
    land_mask,
    interval,
    samples,
    wide_weights,
    wide_firsts,
    wide_seconds,
    tall_weights,
    tall_firsts,
    tall_seconds,
    query_vector,
    query_firsts,
    query_seconds,
):
    wide_all, tall_all, query_all = (
        lax.all_gather(wide_weights.astype(jnp.bfloat16), "grp", axis=0, tiled=True),
        lax.all_gather(tall_weights.astype(jnp.bfloat16), "grp", axis=1, tiled=True),
        lax.all_gather(query_vector.astype(jnp.bfloat16), "grp", axis=0, tiled=True),
    )
    width = wide_all.shape[0]
    heads = HEADS
    head_dim = width // heads
    items, tokens = (fields.shape[0], fields.shape[1])
    outputs = VARS * PIX
    scale = head_dim ** (-0.5)
    cuts = [
        0,
        width,
        2 * width,
        3 * width,
        9 * width,
        12 * width,
        13 * width,
        13 * width + FF,
        13 * width + FF + outputs,
    ]
    agg_key, agg_value, agg_out, modulation, qkv_weight, attn_out, up_weight, head_weight = [
        wide_all[:, cuts[j] : cuts[j + 1]] for j in range(8)
    ]
    embed = tall_all[:outputs].reshape(VARS, PIX, width)
    down_weight = tall_all[outputs:]
    agg_heads = agg_value.reshape(width, heads, head_dim)
    pixels = fields.reshape(items, tokens, VARS, PIX)
    embedded = product("iqvk,vkd->iqvd", pixels, embed).astype(jnp.bfloat16)
    probe = product(
        "dhc,hc->hd", agg_key.reshape(width, heads, head_dim), query_all.reshape(heads, head_dim)
    ).astype(jnp.bfloat16)
    keep = land_mask[:, :, None, :] > 0
    var_scores = jnp.where(keep, product("iqvd,hd->iqhv", embedded, probe) * scale, masked_score)
    var_probs = jax.nn.softmax(var_scores, axis=-1)
    var_probs_low = var_probs.astype(jnp.bfloat16)
    pooled = product("iqhv,iqvd->iqhd", var_probs_low, embedded).astype(jnp.bfloat16)
    gathered = (
        product("iqhd,dhc->iqhc", pooled, agg_heads)
        .reshape(items, tokens, width)
        .astype(jnp.bfloat16)
    )
    residual_a = product("iqd,de->iqe", gathered, agg_out)
    group_lead = lead_features(jnp.arange(3, dtype=jnp.int32), width).astype(jnp.bfloat16)
    group_mod = product("gd,de->ge", group_lead, modulation)
    member = (interval[:, None] == jnp.arange(3, dtype=jnp.int32)[None, :]).astype(jnp.float32)
    modul = precise("ig,ge->ie", member, group_mod).reshape(items, 6, 1, width)
    shift_a, scale_a, gate_a, shift_b, scale_b, gate_b = [modul[:, j] for j in range(6)]
    normed_a, pull_a = jax.vjp(modulate, residual_a, shift_a, scale_a)
    normed_a_low = normed_a.astype(jnp.bfloat16)
    qkv_low = product("iqd,de->iqe", normed_a_low, qkv_weight).astype(jnp.bfloat16)
    query_low = qkv_low[..., :width]
    key_low = qkv_low[..., width : 2 * width]
    value_low = qkv_low[..., 2 * width :]
    query_heads = query_low.reshape(items, tokens, heads, head_dim)
    piece = (
        lax.all_gather(key_low, "seq", axis=1, tiled=True),
        lax.all_gather(value_low, "seq", axis=1, tiled=True),
    )
    highest = jnp.full((items, heads, tokens), masked_score, jnp.float32)
    key_heads = piece[0].reshape(items, -1, heads, head_dim)
    value_heads = piece[1].reshape(items, -1, heads, head_dim)
    scores = product("iqhc,inhc->ihqn", query_heads, key_heads) * scale
    topmost = jnp.maximum(highest, jnp.max(scores, axis=-1))
    probs = jnp.exp(scores - topmost[..., None])
    total = jnp.sum(probs, axis=-1)
    accum = product("ihqn,inhc->ihqc", probs.astype(jnp.bfloat16), value_heads)
    highest, total, accum = (topmost, total, accum)
    attended = (accum / total[..., None]).transpose(0, 2, 1, 3)
    logsum = highest + jnp.log(total)
    attended_low = attended.reshape(items, tokens, width).astype(jnp.bfloat16)
    branch_a = product("iqd,de->iqe", attended_low, attn_out)
    residual_b = residual_a + gate_a * branch_a
    normed_b, pull_b = jax.vjp(modulate, residual_b, shift_b, scale_b)
    normed_b_low = normed_b.astype(jnp.bfloat16)
    expand = product("iqd,df->iqf", normed_b_low, up_weight)
    activated, pull_gelu = jax.vjp(gelu_tanh, expand)
    activated_low = activated.astype(jnp.bfloat16)
    branch_b = product("iqf,fd->iqd", activated_low, down_weight)
    residual_c = residual_b + gate_b * branch_b
    final, pull_final = jax.vjp(layer_norm, residual_c)
    final_low = final.astype(jnp.bfloat16)
    predicted = product("iqd,do->iqo", final_low, head_weight)
    rows_total = tokens * lax.axis_size("seq") // COLS
    position = lax.axis_index("seq") * tokens + jnp.arange(tokens)
    latitude = jnp.pi * (((position // COLS).astype(jnp.float32) + 0.5) / rows_total - 0.5)
    weight = (
        samples.astype(jnp.float32)[:, None, None]
        * jnp.cos(latitude)[None, :, None]
        * land_mask.astype(jnp.float32)
    )
    diff = predicted.reshape(items, tokens, VARS, PIX) - targets.reshape(
        items, tokens, VARS, PIX
    ).astype(jnp.float32)
    loss_part = jnp.sum(weight * jnp.mean(diff * diff, axis=-1))
    loss_sum, weight_sum = lax.psum((loss_part, jnp.sum(weight)), ("grp", "seq"))
    grad_pred = (
        (2.0 / PIX * (weight / weight_sum)[..., None] * diff)
        .reshape(items, tokens, outputs)
        .astype(jnp.bfloat16)
    )
    grad_head = product("iqd,iqo->do", final_low, grad_pred)
    grad_residual = pull_final(product("iqo,do->iqd", grad_pred, head_weight))[0]
    grad_branch_b = (gate_b * grad_residual).astype(jnp.bfloat16)
    grad_gate_b = jnp.sum(grad_residual * branch_b, axis=1)
    grad_down = product("iqf,iqd->fd", activated_low, grad_branch_b)
    grad_expand = pull_gelu(product("iqd,fd->iqf", grad_branch_b, down_weight))[0].astype(
        jnp.bfloat16
    )
    grad_up = product("iqd,iqf->df", normed_b_low, grad_expand)
    back_b = pull_b(product("iqf,df->iqd", grad_expand, up_weight))
    grad_residual = grad_residual + back_b[0]
    grad_branch_a = (gate_a * grad_residual).astype(jnp.bfloat16)
    grad_gate_a = jnp.sum(grad_residual * branch_a, axis=1)
    grad_attn_out = product("iqd,iqe->de", attended_low, grad_branch_a)
    grad_attended = product("iqe,de->iqd", grad_branch_a, attn_out).astype(jnp.bfloat16)
    grad_heads = grad_attended.reshape(items, tokens, heads, head_dim)
    delta = jnp.sum(grad_heads.astype(jnp.float32) * attended, axis=-1).transpose(0, 2, 1)
    own_keys = key_low.reshape(items, tokens, heads, head_dim)
    own_values = value_low.reshape(items, tokens, heads, head_dim)
    logsum_all, delta_all = (
        lax.all_gather(logsum.transpose(0, 2, 1), "seq", axis=1, tiled=True),
        lax.all_gather(delta.transpose(0, 2, 1), "seq", axis=1, tiled=True),
    )
    piece = (
        lax.all_gather(query_low, "seq", axis=1, tiled=True),
        lax.all_gather(grad_attended, "seq", axis=1, tiled=True),
    )
    query_piece = piece[0].reshape(items, -1, heads, head_dim)
    grad_piece = piece[1].reshape(items, -1, heads, head_dim)
    logsum_piece = logsum_all.transpose(0, 2, 1)
    delta_piece = delta_all.transpose(0, 2, 1)
    probs_low, grad_scores = block_grads(
        query_piece, own_keys, own_values, grad_piece, logsum_piece, delta_piece, scale
    )
    grad_key_acc = product("ihqn,iqhc->inhc", grad_scores, query_piece) * scale
    grad_value_acc = product("ihqn,iqhc->inhc", probs_low, grad_piece)
    grad_keys = grad_key_acc
    grad_values = grad_value_acc
    grad_keys = grad_keys.reshape(items, tokens, width)
    grad_values = grad_values.reshape(items, tokens, width)
    piece = (
        lax.all_gather(key_low, "seq", axis=1, tiled=True),
        lax.all_gather(value_low, "seq", axis=1, tiled=True),
    )
    key_heads = piece[0].reshape(items, -1, heads, head_dim)
    value_heads = piece[1].reshape(items, -1, heads, head_dim)
    probs_low, grad_scores = block_grads(
        query_heads, key_heads, value_heads, grad_heads, logsum, delta, scale
    )
    grad_query_acc = product("ihqn,inhc->iqhc", grad_scores, key_heads) * scale
    grad_qkv = jnp.concatenate(
        [grad_query_acc.reshape(items, tokens, width), grad_keys, grad_values], axis=-1
    ).astype(jnp.bfloat16)
    grad_qkv_weight = product("iqd,iqe->de", normed_a_low, grad_qkv)
    back_a = pull_a(product("iqe,de->iqd", grad_qkv, qkv_weight))
    grad_first = (grad_residual + back_a[0]).astype(jnp.bfloat16)
    grad_mod = jnp.stack(
        [
            back_a[1][:, 0],
            back_a[2][:, 0],
            grad_gate_a,
            back_b[1][:, 0],
            back_b[2][:, 0],
            grad_gate_b,
        ],
        axis=1,
    ).reshape(items, 6 * width)
    grad_group_mod = precise("ig,ie->ge", member, grad_mod)
    grad_modulation = precise("gd,ge->de", group_lead.astype(jnp.float32), grad_group_mod)
    grad_agg_out = product("iqd,iqe->de", gathered, grad_first)
    grad_gathered = (
        product("iqe,de->iqd", grad_first, agg_out)
        .astype(jnp.bfloat16)
        .reshape(items, tokens, heads, head_dim)
    )
    grad_agg_value = product("iqhd,iqhc->dhc", pooled, grad_gathered).reshape(width, width)
    grad_pooled = product("iqhc,dhc->iqhd", grad_gathered, agg_heads).astype(jnp.bfloat16)
    grad_var_probs = product("iqhd,iqvd->iqhv", grad_pooled, embedded)
    grad_embedded = product("iqhv,iqhd->iqvd", var_probs_low, grad_pooled)
    grad_var_scores = (
        var_probs * (grad_var_probs - jnp.sum(var_probs * grad_var_probs, axis=-1, keepdims=True))
    ).astype(jnp.bfloat16)
    grad_embedded = (
        grad_embedded + product("iqhv,hd->iqvd", grad_var_scores, probe) * scale
    ).astype(jnp.bfloat16)
    grad_probe = product("iqhv,iqvd->hd", grad_var_scores, embedded) * scale
    grad_embed = product("iqvk,iqvd->vkd", pixels, grad_embedded).reshape(outputs, width)
    query_heads_vec = query_all.astype(jnp.float32).reshape(heads, head_dim)
    grad_agg_key = (grad_probe.T[:, :, None] * query_heads_vec[None, :, :]).reshape(width, width)
    grad_query_vec = precise(
        "dhc,hd->hc", agg_key.astype(jnp.float32).reshape(width, heads, head_dim), grad_probe
    ).reshape(width)
    wide_grad = jnp.concatenate(
        [
            grad_agg_key,
            grad_agg_value,
            grad_agg_out,
            grad_modulation,
            grad_qkv_weight,
            grad_attn_out,
            grad_up,
            grad_head,
        ],
        axis=1,
    )
    tall_grad = jnp.concatenate([grad_embed, grad_down], axis=0)
    wide_grad, tall_grad, query_grad = (
        lax.psum_scatter(
            wide_grad.astype(jnp.bfloat16), "grp", scatter_dimension=0, tiled=True
        ).astype(jnp.float32),
        lax.psum_scatter(
            tall_grad.astype(jnp.bfloat16), "grp", scatter_dimension=1, tiled=True
        ).astype(jnp.float32),
        lax.psum_scatter(
            grad_query_vec.astype(jnp.bfloat16), "grp", scatter_dimension=0, tiled=True
        ).astype(jnp.float32),
    )
    wide_grad, tall_grad, query_grad = (
        lax.psum(wide_grad.astype(jnp.bfloat16), "seq").astype(jnp.float32),
        lax.psum(tall_grad.astype(jnp.bfloat16), "seq").astype(jnp.float32),
        lax.psum(query_grad.astype(jnp.bfloat16), "seq").astype(jnp.float32),
    )
    squares = (
        jnp.sum(wide_grad * wide_grad)
        + jnp.sum(tall_grad * tall_grad)
        + jnp.sum(query_grad * query_grad)
    )
    grad_norm = jnp.sqrt(lax.psum(squares, "grp"))
    factor = jnp.minimum(1.0, clip_limit / (grad_norm + 1e-06))
    wide_out = adamw_update(wide_weights, wide_firsts, wide_seconds, wide_grad * factor)
    tall_out = adamw_update(tall_weights, tall_firsts, tall_seconds, tall_grad * factor)
    query_out = adamw_update(query_vector, query_firsts, query_seconds, query_grad * factor)
    return (loss_sum, weight_sum, grad_norm) + wide_out + tall_out + query_out


def solution(mesh):
    placed = (
        P("grp", "seq", None),
        P("grp", "seq", None),
        P("grp", "seq", None),
        P("grp"),
        P("grp"),
        P("grp", None),
        P("grp", None),
        P("grp", None),
        P(None, "grp"),
        P(None, "grp"),
        P(None, "grp"),
        P("grp"),
        P("grp"),
        P("grp"),
    )
    return jax.shard_map(
        per_device,
        mesh=mesh,
        in_specs=placed,
        out_specs=(
            P(),
            P(),
            P(),
            P("grp", None),
            P("grp", None),
            P("grp", None),
            P("grp", None),
            P(None, "grp"),
            P(None, "grp"),
            P(None, "grp"),
            P(None, "grp"),
            P("grp"),
            P("grp"),
            P("grp"),
            P("grp"),
        ),
        check_vma=False,
    )
```

profile of v0, /device:TPU:0, one launch (start us, length us, event | category | flops | bytes accessed | tf_op | source)
XLA Modules:
  0.0 824.3 jit_solution(13738507496976937190)
XLA Ops:
  22.9 12.4 %all-gather.9.cloned.1.call-done = bf16[2640,384]{0,1:T(8,128)(2,1)} async-done(((bf16[2640,96]{0,1:T(8,128)(2,1)}), bf16[2640,384]{0,1:T(8,128)(2,1)}) %all-gather.9.cloned.1.call-update) | async-done | bytes 2027536 | tf_op jit(solution)/shard_map/all_gather | solution.py:92
  38.0 14.3 %convert_bitcast_fusion = bf16[2,256,69,384]{1,3,0,2:T(8,128)(2,1)} fusion(bf16[69,16,384,1]{2,1,3,0:T(8,128)(2,1)S(1)} %bitcast.248, bf16[2,256,69,16]{1,3,2,0:T(8,128)(2,1)S(1)} %bitcast.238), kind=kOutput, calls=%fused_computation.2 | convolution fusion | flops 447676416 | bytes 29110272 | tf_op jit(solution)/shard_map/iqvk,vkd->iqvd/dot_general | solution.py:25
  52.3 35.8 %copy.211 = bf16[2,256,69,384]{3,2,1,0:T(8,128)(2,1)} copy(bf16[2,256,69,384]{1,3,0,2:T(8,128)(2,1)} %convert_bitcast_fusion) | data formatting | bytes 54263808 | tf_op jit(solution)/shard_map/convert_element_type | solution.py:119
  89.6 10.6 %fusion.143 = (f32[2,256,6]{1,2,0:T(8,128)S(1)}, f32[2,256,6,69]{1,2,3,0:T(8,128)S(1)}) fusion(bf16[2,256,69,384]{1,3,0,2:T(8,128)(2,1)} %convert_bitcast_fusion, bf16[6,1,384]{2,1,0:T(2,128)(2,1)S(1)} %fusion.147, pred[2,256,69]{1,2,0:T(8,128)(4,1)S(1)} %copy.205), kind=kOutput, calls=%fused_computation.234 | convolution fusion | flops 163424256 | bytes 28032000 | tf_op jit(solution)/shard_map/iqvd,hd->iqhv/dot_general | solution.py:25
  103.3 12.2 %fusion.148 = bf16[2,256,6,384]{3,2,1,0:T(8,128)(2,1)S(1)} fusion(bf16[2,256,6,69]{3,2,1,0:T(8,128)(2,1)S(1)} %copy.210, bf16[2,256,69,384]{3,2,1,0:T(8,128)(2,1)} %copy.211), kind=kOutput, calls=%fused_computation.239 | convolution fusion | flops 162791424 | bytes 29915136 | tf_op jit(solution)/shard_map/iqhv,iqvd->iqhd/dot_general | solution.py:25
  125.1 59.5 %all-gather.11.cloned.1.call-done = bf16[2,2048,384]{2,1,0:T(8,128)(2,1)} async-done(((bf16[2,256,384]{2,1,0:T(8,128)(2,1)}), bf16[2,2048,384]{2,1,0:T(8,128)(2,1)}) %all-gather.11.cloned.1.call-update) | async-done | bytes 3145744 | tf_op jit(solution)/shard_map/all_gather | solution.py:147
  189.3 12.1 %multiply_reduce_fusion = (f32[2,6,256]{2,1,0:T(8,128)S(1)}, f32[2,6,256,2048]{3,2,1,0:T(8,128)}) fusion(bf16[2,256,6,64]{1,3,2,0:T(8,128)(2,1)S(1)} %bitcast.256, bf16[2,2048,6,64]{1,3,2,0:T(8,128)(2,1)} %bitcast.240), kind=kOutput, calls=%fused_computation.16 | convolution fusion | flops 817886208 | bytes 28717056 | tf_op jit(solution)/shard_map/iqhc,inhc->ihqn/dot_general | solution.py:25
  201.5 10.8 %fusion.9 = f32[2,6,256]{2,1,0:T(8,128)S(1)} fusion(f32[2,6,256,2048]{3,2,1,0:T(8,128)} %get-tuple-element.128, f32[2,6,256]{2,1,0:T(8,128)S(1)} %broadcast_maximum_fusion), kind=kLoop, calls=%fused_computation.13 | loop fusion | flops 18871296 | bytes 25190400 | tf_op jit(solution)/shard_map/reduce_sum | solution.py:156
  212.3 33.4 %all-gather.13.cloned.1.call-done = bf16[2,2048,384]{2,1,0:T(8,128)(2,1)} async-done(((bf16[2,256,384]{2,1,0:T(8,128)(2,1)}), bf16[2,2048,384]{2,1,0:T(8,128)(2,1)}) %all-gather.13.cloned.1.call-update) | async-done | bytes 3145744 | tf_op jit(solution)/shard_map/all_gather | solution.py:148
  250.4 12.8 %fusion.145 = (bf16[2,256,6,64]{1,3,2,0:T(8,128)(2,1)S(1)}, f32[2,256,6,64]{1,3,2,0:T(8,128)}) fusion(f32[2,256,6]{1,2,0:T(8,128)S(1)} %bitcast.275, bf16[2,2048,6,64]{1,3,2,0:T(8,128)(2,1)} %bitcast.254, f32[2,6,256,2048]{3,2,1,0:T(8,128)} %get-tuple-element.128, f32[2,6,256]{2,1,0:T(8,128)S(1)} %broadcast_maximum_fusion), kind=kOutput, calls=%fused_computation.236 | convolution fusion | flops 824573952 | bytes 29515776 | tf_op jit(solution)/shard_map/ihqn,inhc->ihqc/dot_general | solution.py:25
  278.5 41.0 %all-reduce.2 = (f32[]{:T(128)}, f32[]{:T(128)}) all-reduce(f32[]{:T(128)} %get-tuple-element.82, f32[]{:T(128)} %get-tuple-element.81), channel_id=1, replica_groups=mesh['grp'=4,'seq'=8] {'grp','seq'}, use_global_device_ids=true, to_apply=%region_12.13 | all-reduce | flops 2 | bytes 16 | tf_op jit(solution)/shard_map/psum | solution.py:186
  341.7 16.3 %fusion.68 = bf16[2,6,64,256]{3,2,1,0:T(8,128)(2,1)} fusion(bf16[2,2048,6,64]{1,3,2,0:T(8,128)(2,1)} %bitcast.241, f32[2,6,256,2048]{3,2,1,0:T(8,128)} %get-tuple-element.128, f32[2,6,256]{2,1,0:T(8,128)S(1)} %bitcast.277, f32[2,6,256]{2,1,0:T(8,128)S(1)} %log_add_fusion, bf16[2,256,6,64]{1,3,2,0:T(8,128)(2,1)S(1)} %bitcast.263, ...), kind=kOutput, calls=%fused_computation.87 | convolution fusion | flops 1642463232 | bytes 32268288 | tf_op jit(solution)/shard_map/ihqn,inhc->iqhc/dot_general | solution.py:25
  370.2 31.5 %all_gather.37 = f32[2,2048,6]{1,2,0:T(8,128)S(1)} all-gather(f32[2,256,6]{1,2,0:T(8,128)S(1)} %multiply_reduce_fusion.7), channel_id=1, replica_groups=mesh['grp'=4,'seq'=8] {'seq'}, dimensions={1}, use_global_device_ids=true | all-gather | bytes 110592 | tf_op jit(solution)/shard_map/all_gather | solution.py:213
  401.7 30.5 %all_gather.35 = f32[2,2048,6]{1,2,0:T(8,128)S(1)} all-gather(f32[2,256,6]{1,2,0:T(8,128)S(1)} %bitcast_add_fusion), channel_id=1, replica_groups=mesh['grp'=4,'seq'=8] {'seq'}, dimensions={1}, use_global_device_ids=true | all-gather | bytes 110592 | tf_op jit(solution)/shard_map/all_gather | solution.py:212
  436.9 10.1 %fusion.149 = f32[2,6,2048,256]{3,2,1,0:T(8,128)} fusion(bf16[2,2048,6,64]{1,3,2,0:T(8,128)(2,1)S(1)} %bitcast.245, bf16[2,256,6,64]{1,3,2,0:T(8,128)(2,1)S(1)} %bitcast.259), kind=kOutput, calls=%fused_computation.240 | convolution fusion | flops 805306368 | bytes 28704768 | tf_op jit(solution)/shard_map/iqhc,inhc->ihqn/dot_general | solution.py:25
  451.8 10.9 %fusion.70 = bf16[2,6,64,256]{3,2,1,0:T(8,128)(2,1)S(1)} fusion(bf16[2,2048,6,64]{1,3,2,0:T(8,128)(2,1)} %bitcast.242, f32[2,6,2048,256]{3,2,1,0:T(8,128)} %fusion.149, f32[2,6,2048]{2,1,0:T(8,128)S(1)} %bitcast.252), kind=kOutput, calls=%fused_computation.89 | convolution fusion | flops 824377344 | bytes 28803072 | tf_op jit(solution)/shard_map/ihqn,iqhc->inhc/dot_general | solution.py:25
  462.7 15.4 %fusion.69 = bf16[2,6,64,256]{3,2,1,0:T(8,128)(2,1)} fusion(bf16[2,2048,6,64]{1,3,2,0:T(8,128)(2,1)} %bitcast.244, f32[2,6,2048,256]{3,2,1,0:T(8,128)} %fusion.149, f32[2,6,2048]{2,1,0:T(8,128)S(1)} %bitcast.276, f32[2,6,2048]{2,1,0:T(8,128)S(1)} %bitcast.253, bf16[2,2048,6,64]{1,3,2,0:T(8,128)(2,1)} %bitcast.243, bf16[2,256,6,64]{1,3,2,0:T(8,128)(2,1)} %bitcast.271), kind=kOutput, calls=%fused_computation.88 | convolution fusion | flops 1642463232 | bytes 32440320 | tf_op jit(solution)/shard_map/ihqn,iqhc->inhc/dot_general | solution.py:25
  490.9 21.5 %fusion.23 = f32[2,256,69,384]{3,2,1,0:T(8,128)} fusion(bf16[2,256,6,69]{3,2,1,0:T(8,128)(2,1)S(1)} %copy-done.6, bf16[2,256,6,384]{3,1,0,2:T(8,128)(2,1)S(1)} %convert_bitcast_fusion.1), kind=kOutput, calls=%fused_computation.33 | convolution fusion | flops 162791424 | bytes 57047040 | tf_op jit(solution)/shard_map/iqhv,iqhd->iqvd/dot_general | solution.py:25
  512.4 15.3 %fusion.25 = f32[2,256,6,69]{3,2,1,0:T(8,128)} fusion(bf16[2,256,69,384]{3,2,1,0:T(8,128)(2,1)} %copy.211, bf16[2,256,6,384]{3,1,0,2:T(8,128)(2,1)S(1)} %convert_bitcast_fusion.1), kind=kOutput, calls=%fused_computation.35 | convolution fusion | flops 162791424 | bytes 30339072 | tf_op jit(solution)/shard_map/iqhd,iqvd->iqhv/dot_general | solution.py:25
  534.4 37.4 %bitcast_convert_fusion = bf16[69,384,16]{1,2,0:T(8,128)(2,1)S(1)} fusion(bf16[2,256,69,16]{1,3,2,0:T(8,128)(2,1)S(1)} %bitcast.239, f32[2,256,69,384]{3,2,1,0:T(8,128)} %fusion.23, bf16[2,256,6,69]{1,2,3,0:T(8,128)(2,1)} %multiply_convert_fusion.13, bf16[6,1,384]{2,1,0:T(2,128)(2,1)S(1)} %copy-done.48), kind=kOutput, calls=%fused_computation.69 | convolution fusion | flops 638023680 | bytes 56670720 | tf_op jit(solution)/shard_map/iqvk,iqvd->vkd/dot_general | solution.py:25
  578.8 13.4 %fusion.87 = f32[6,384]{1,0:T(8,128)S(1)} fusion(bf16[2,256,6,69]{1,2,3,0:T(8,128)(2,1)S(1)} %copy-done.11, bf16[2,256,69,384]{1,3,0,2:T(8,128)(2,1)} %convert_bitcast_fusion), kind=kOutput, calls=%fused_computation.107 | convolution fusion | flops 162793728 | bytes 27565056 | tf_op jit(solution)/shard_map/iqhv,iqvd->hd/dot_general | solution.py:25
  616.0 53.3 %reduce-scatter.5.cloned.1.call-done = bf16[96,7632]{1,0:T(8,128)(2,1)} async-done(((bf16[384,7632]{1,0:T(8,128)(2,1)}), bf16[96,7632]{1,0:T(8,128)(2,1)}) %reduce-scatter.5.cloned.1.call-update) | async-done | bytes 1465360 | tf_op jit(solution)/shard_map/reduce_scatter | solution.py:299
  680.4 22.9 %psum.46 = bf16[96]{0:T(256)(128)(2,1)S(1)} all-reduce(bf16[96]{0:T(256)(128)(2,1)S(1)} %dynamic-slice.2), channel_id=1, replica_groups=mesh['grp'=4,'seq'=8] {'seq'}, use_global_device_ids=true, to_apply=%region_36.37 | all-reduce | flops 96 | bytes 384 | tf_op jit(solution)/shard_map/psum | solution.py:312
  704.0 73.3 %all-reduce.6.cloned.1.call-done = (bf16[96,7632]{1,0:T(8,128)(2,1)}, bf16[2640,96]{1,0:T(8,128)(2,1)}) async-done(((bf16[96,7632]{1,0:T(8,128)(2,1)}, bf16[2640,96]{1,0:T(8,128)(2,1)}), (bf16[96,7632]{1,0:T(8,128)(2,1)}, bf16[2640,96]{1,0:T(8,128)(2,1)})) %all-reduce.6.cloned.1.call-update) | async-done | bytes 1972240 | tf_op jit(solution)/shard_map/psum | solution.py:310
  (298 shorter events, 197.3 us)
Async XLA Ops:
  7.2 30.8 %copy-start = (bf16[2,256,1104]{1,2,0:T(8,128)(2,1)S(1)}, bf16[2,256,1104]{1,2,0:T(8,128)(2,1)}, u32[]{:S(2)}) copy-start(bf16[2,256,1104]{1,2,0:T(8,128)(2,1)} %param.14) | copy-start | bytes 3391492
  7.2 28.1 %all-gather.9.cloned.1.call-start = ((), (), s32[]{:S(2)}) async-start(), calls=%async_computation.3 | async-start | bytes 2580480 | tf_op jit(solution)/shard_map/all_gather | solution.py:92
  9.4 13.2 %copy-start.31 = (s32[2,256,69]{1,0,2:T(2,128)S(1)}, s32[2,256,69]{1,0,2:T(2,128)}, u32[]{:S(2)}) copy-start(s32[2,256,69]{1,0,2:T(2,128)} %param.16) | copy-start | bytes 423940
  9.4 78.6 %all-gather.7.cloned.1.call-start = ((), (), s32[]{:S(2)}) async-start(), calls=%async_computation.2 | async-start | bytes 7372800 | tf_op jit(solution)/shard_map/all_gather | solution.py:91
  12.6 171.9 %all-gather.11.cloned.1.call-start = ((), (), s32[]{:S(2)}) async-start(), calls=%async_computation.4 | async-start | bytes 3538944 | tf_op jit(solution)/shard_map/all_gather | solution.py:147
  22.9 95.6 %copy-start.49 = (f32[3,192]{1,0:T(4,128)}, f32[3,192]{1,0:T(4,128)S(1)}, u32[]{:S(2)}) copy-start(f32[3,192]{1,0:T(4,128)S(1)} %get-tuple-element.119) | copy-start | bytes 6916
  22.9 95.6 %copy-start.51 = (f32[3,192]{1,0:T(4,128)}, f32[3,192]{1,0:T(4,128)S(1)}, u32[]{:S(2)}) copy-start(f32[3,192]{1,0:T(4,128)S(1)} %get-tuple-element.120) | copy-start | bytes 6916
  103.0 12.4 %copy-start.5 = (bf16[2,256,6,69]{3,2,1,0:T(8,128)(2,1)}, bf16[2,256,6,69]{3,2,1,0:T(8,128)(2,1)S(1)}, u32[]{:S(2)}) copy-start(bf16[2,256,6,69]{3,2,1,0:T(8,128)(2,1)S(1)} %copy.210) | copy-start | bytes 1271812
  103.3 12.2 %copy-start.33 = (bf16[384,384]{0,1:T(8,128)(2,1)}, bf16[384,384]{0,1:T(8,128)(2,1)S(1)}, u32[]{:S(2)}) copy-start(bf16[384,384]{0,1:T(8,128)(2,1)S(1)} %copy.213) | copy-start | bytes 884740
  118.2 366.3 %copy-start.3 = (f32[2,256,384]{2,1,0:T(8,128)}, f32[2,256,384]{2,1,0:T(8,128)S(1)}, u32[]{:S(2)}) copy-start(f32[2,256,384]{2,1,0:T(8,128)S(1)} %get-tuple-element.126) | copy-start | bytes 2359300
  123.8 121.9 %all-gather.13.cloned.1.call-start = ((), (), s32[]{:S(2)}) async-start(), calls=%async_computation.5 | async-start | bytes 3538944 | tf_op jit(solution)/shard_map/all_gather | solution.py:148
  124.4 241.0 %all-gather.15.cloned.1.call-start = ((), (), s32[]{:S(2)}) async-start(), calls=%async_computation.6 | async-start | bytes 3538944 | tf_op jit(solution)/shard_map/all_gather | solution.py:216
  125.0 322.0 %all-gather.17.cloned.1.call-start = ((), (), s32[]{:S(2)}) async-start(), calls=%async_computation.7 | async-start | bytes 3538944 | tf_op jit(solution)/shard_map/all_gather | solution.py:217
  125.1 140.9 %copy-start.53 = (f32[2,384]{1,0:T(2,128)}, f32[2,384]{1,0:T(2,128)S(1)}, u32[]{:S(2)}) copy-start(f32[2,384]{1,0:T(2,128)S(1)} %get-tuple-element.141) | copy-start | bytes 9220
  335.8 278.0 %reduce-scatter.7.cloned.1.call-start = ((), (), s32[]{:S(2)}) async-start(), calls=%async_computation.9 | async-start | bytes 2580480
  578.8 13.5 %copy-start.21 = (bf16[2,256,6,64]{1,3,2,0:T(8,128)(2,1)S(1)}, bf16[2,256,6,64]{1,3,2,0:T(8,128)(2,1)}, u32[]{:S(2)}) copy-start(bf16[2,256,6,64]{1,3,2,0:T(8,128)(2,1)} %copy-done.20) | copy-start | bytes 1179652
  578.8 90.5 %reduce-scatter.5.cloned.1.call-start = ((), (), s32[]{:S(2)}) async-start(), calls=%async_computation.8 | async-start | bytes 7372800 | tf_op jit(solution)/shard_map/reduce_scatter | solution.py:299
  593.0 11.3 %copy-start.55 = (f32[2,384]{1,0:T(2,128)S(1)}, f32[2,384]{1,0:T(2,128)}, u32[]{:S(2)}) copy-start(f32[2,384]{1,0:T(2,128)} %get-tuple-element.80) | copy-start | bytes 9220
  593.0 11.4 %copy-start.66 = (s32[2]{0:T(128)S(1)}, s32[2]{0:T(128)}, u32[]{:S(2)}) copy-start(s32[2]{0:T(128)} %param.17) | copy-start | bytes 28
  593.0 11.7 %copy-start.50 = (f32[3,192]{1,0:T(4,128)S(1)}, f32[3,192]{1,0:T(4,128)}, u32[]{:S(2)}) copy-start(f32[3,192]{1,0:T(4,128)} %copy-done.49) | copy-start | bytes 6916
  593.0 11.7 %copy-start.52 = (f32[3,192]{1,0:T(4,128)S(1)}, f32[3,192]{1,0:T(4,128)}, u32[]{:S(2)}) copy-start(f32[3,192]{1,0:T(4,128)} %copy-done.51) | copy-start | bytes 6916
  613.7 55.6 %copy-start.16 = (f32[2640,96]{0,1:T(8,128)S(1)}, f32[2640,96]{0,1:T(8,128)}, u32[]{:S(2)}) copy-start(f32[2640,96]{0,1:T(8,128)} %param.22) | copy-start | bytes 3041284
  613.7 163.6 %all-reduce.6.cloned.1.call-start = ((), (), s32[]{:S(2)}) async-start(), calls=%async_computation.10 | async-start | bytes 4300800 | tf_op jit(solution)/shard_map/psum | solution.py:310
  777.3 17.3 %copy-start.26 = (bf16[2640,96]{1,0:T(8,128)(2,1)S(1)}, bf16[2640,96]{1,0:T(8,128)(2,1)}, u32[]{:S(2)}) copy-start(bf16[2640,96]{1,0:T(8,128)(2,1)} %get-tuple-element.86) | copy-start | bytes 1520644
  (54 other events, 245.9 us)
Sparse Core Ops, SparseCore 0:
  10.2 25.0 all-gather.8
  37.4 44.1 all-gather.6
  123.9 60.5 all-gather.10
  186.6 59.0 all-gather.12
  247.7 60.6 all-gather.14
  335.9 62.2 all-gather.16
  578.9 31.1 reduce-scatter.6
  613.8 55.4 reduce-scatter.4
  673.6 103.6 all-reduce.5
where the time goes:
time: 836 us; the launch traced here: 824 us
  matrix products  260 us (31%)
  waiting for transfers between devices  233 us (28%)
  blocking collectives  147 us (18%)
  local copies, waits for them, and re-layouts  110 us (13%)
  other arithmetic  54.1 us (6%)
  between operations  20.2 us (2%)
    dot_general x36, matrix products, product(): return jnp.einsum(spec, left, right, preferred_element_type=jnp.float32)  255 us
    psum x1, waiting for transfers between devices, per_device(): lax.psum(wide_grad.astype(jnp.bfloat16), 'seq').astype(jnp.float32)  73.3 us
    all_gather x1, waiting for transfers between devices, per_device(): lax.all_gather(key_low, 'seq', axis=1, tiled=True)  59.5 us
    reduce_scatter x1, waiting for transfers between devices, per_device(): lax.psum_scatter(wide_grad.astype(jnp.bfloat16), 'grp', scatter_dimension...  53.3 us
    psum x1, blocking collectives, per_device(): lax.psum((loss_part, jnp.sum(weight)), ('grp', 'seq'))  41 us
    convert_element_type x1, local copies, waits for them, and re-layouts, per_device(): embedded = product('iqvk,vkd->iqvd', pixels, embed).astype(jnp.bfloat16)  35.8 us
    all_gather x1, waiting for transfers between devices, per_device(): lax.all_gather(value_low, 'seq', axis=1, tiled=True)  33.4 us
    all_gather x1, blocking collectives, per_device(): lax.all_gather(delta.transpose(0, 2, 1), 'seq', axis=1, tiled=True)  31.5 us
  transfers between devices with their start and end apart: 9, of which 5 were waited for; matrix products, arithmetic and copies ran while one was open for 27% of the time, Pallas kernels for 0%

commit v1 on v0

v1 whole, which is shorter than its diff:
```python
import functools

import jax
import jax.numpy as jnp
from jax import lax
from jax.experimental import pallas as pl
from jax.experimental.pallas import tpu as pltpu
from jax.sharding import PartitionSpec as P

D = 384
HEADS = 6
HEAD = 64
FF = 1536
VARS = 69
PIX = 16
OUT = VARS * PIX
OUTP = 1152
COLS = 128
STEP = 5
CUTS = 4
SCALE = HEAD**-0.5
LOG2E = 1.4426950408889634

beta_first = 0.5
beta_second = 0.5
learn_rate = 0.1
decay_rate = 0.01
adam_epsilon = 1e-08
clip_limit = 0.05
norm_epsilon = 1e-06
masked_score = -1e30

F32 = jnp.float32
BF16 = jnp.bfloat16
LIMIT = 50 * 1024 * 1024


def dot(left, right, a, b):
    return lax.dot_general(left, right, (((a,), (b,)), ((), ())), preferred_element_type=F32)


def nn(left, right):
    return dot(left, right, 1, 0)


def nt(left, right):
    return dot(left, right, 1, 1)


def tn(left, right):
    return dot(left, right, 0, 0)


def iota(shape, dim):
    return lax.broadcasted_iota(jnp.int32, shape, dim)


def half_low(shape):
    return iota(shape, len(shape) - 1) < HEAD


def swap_halves(tile):
    return pltpu.roll(tile, HEAD, 1)


def spread():
    return iota((128, OUT), 1) // PIX == iota((128, OUT), 0)


def place():
    grp = lax.axis_index("grp")
    seq = lax.axis_index("seq")
    return grp, seq


def call(kernel, outs, grid=(), in_specs=None, out_specs=None, scratch=(), flops=0, limit=LIMIT):
    kw = {}
    if in_specs is not None:
        kw["in_specs"] = in_specs
    if out_specs is not None:
        kw["out_specs"] = out_specs
    return pl.pallas_call(
        kernel,
        out_shape=outs,
        grid=grid,
        scratch_shapes=list(scratch),
        compiler_params=pltpu.CompilerParams(vmem_limit_bytes=limit),
        **kw,
    )


def whole():
    return pl.BlockSpec(memory_space=pltpu.VMEM)


def smem():
    return pl.BlockSpec(memory_space=pltpu.SMEM)


def sds(shape, dtype):
    return jax.ShapeDtypeStruct(shape, dtype)


def standardize(x):
    centered = x - jnp.mean(x, axis=-1, keepdims=True)
    rstd = lax.rsqrt(jnp.mean(centered * centered, axis=-1, keepdims=True) + norm_epsilon)
    return centered * rstd, rstd


def standardize_back(grad, normed, rstd):
    return rstd * (
        grad
        - jnp.mean(grad, axis=-1, keepdims=True)
        - normed * jnp.mean(grad * normed, axis=-1, keepdims=True)
    )


def gelu_parts(x):
    k = 0.7978845608028654
    inner = k * (x + 0.044715 * x * x * x)
    t = jnp.tanh(inner)
    value = 0.5 * x * (1.0 + t)
    slope = 0.5 * (1.0 + t) + 0.5 * x * (1.0 - t * t) * k * (1.0 + 3 * 0.044715 * x * x)
    return value, slope


def pack_first(wide_ref, tall_ref, query_ref, out_ref):
    rows = wide_ref.shape[0]
    out_ref[:, : 3 * D] = wide_ref[...].astype(BF16)
    out_ref[:, 3 * D : 3 * D + OUT] = tall_ref[...].T.astype(BF16)
    eye = iota((rows, rows), 0) == iota((rows, rows), 1)
    column = jnp.sum(jnp.where(eye, query_ref[...], 0.0), axis=1, keepdims=True)
    tail = jnp.where(iota((rows, OUTP - OUT), 1) == 0, column, 0.0)
    out_ref[:, 3 * D + OUT :] = tail.astype(BF16)


def pack_rest(wide_ref, tall_ref, lead_ref, qkv_ref, late_ref, mod_ref):
    rows = wide_ref.shape[0]
    grp, _ = place()
    base = 3 * D
    low = half_low((rows, 128))
    for j in range(HEADS // 2):
        k = wide_ref[:, base + 6 * D + D + j * 128 : base + 6 * D + D + (j + 1) * 128]
        v = wide_ref[:, base + 6 * D + 2 * D + j * 128 : base + 6 * D + 2 * D + (j + 1) * 128]
        qkv_ref[:, (2 * j) * 128 : (2 * j + 1) * 128] = jnp.where(low, k, swap_halves(v)).astype(
            BF16
        )
        qkv_ref[:, (2 * j + 1) * 128 : (2 * j + 2) * 128] = jnp.where(
            low, swap_halves(k), v
        ).astype(BF16)
    qkv_ref[:, 2 * D :] = wide_ref[:, base + 6 * D : base + 7 * D].astype(BF16)
    start = 12 * D
    late_ref[:, : D + FF + OUT] = wide_ref[:, start:].astype(BF16)
    late_ref[:, D + FF + OUT : D + FF + OUTP] = jnp.zeros((rows, OUTP - OUT), BF16)
    late_ref[:, D + FF + OUTP :] = tall_ref[OUT:, :].T.astype(BF16)
    lead = lead_ref[pl.ds(pl.multiple_of(grp * rows, 16), rows), :].astype(F32)
    mod = wide_ref[:, base : base + 6 * D].astype(BF16).astype(F32)
    parts = [jnp.sum(lead[:, g : g + 1] * mod, axis=0, keepdims=True) for g in range(3)]
    mod_ref[...] = jnp.zeros_like(mod_ref)
    for g in range(3):
        mod_ref[g : g + 1, :] = parts[g]


def assemble(target, blocks, grp, lo, hi):
    for j, ref in enumerate(blocks):
        rows = ref.shape[0]
        at = pl.multiple_of(jnp.bitwise_xor(grp, j) * rows, 16)
        target[pl.ds(at, rows), :] = ref[:, lo:hi]


def prepare(*refs):
    blocks, (agg_ref, embed_ref, score_ref, fused_ref, probe_ref) = refs[:-5], refs[-5:]
    grp, _ = place()
    assemble(agg_ref, blocks, grp, 0, 3 * D)
    assemble(embed_ref, blocks, grp, 3 * D, 3 * D + OUTP)
    query = embed_ref[:, OUT : OUT + 1].astype(F32)
    picked = jnp.where(iota((D, 128), 1) == iota((D, 128), 0) // HEAD, query, 0.0).astype(BF16)
    probe = nn(agg_ref[:, :D], picked).astype(BF16)
    probe_ref[...] = probe
    embed = embed_ref[:, :OUT]
    rows = tn(probe, embed) * SCALE
    mine = spread()
    for h in range(HEADS):
        score_ref[h * 128 : (h + 1) * 128, :] = jnp.where(mine, rows[h : h + 1, :], 0.0).astype(
            BF16
        )
    fused_ref[...] = tn(agg_ref[:, D : 2 * D], embed).astype(BF16)


def widen_mask(mask_ref, scratch):
    scratch[...] = jnp.full(scratch.shape, -1, jnp.int32)
    scratch[:, :VARS] = mask_ref[0]
    value = scratch[...]
    return value > 0, value < 0


def aggregate(group, *refs):
    (interval, fields_ref, mask_ref, score_ref, fused_ref, agg_ref) = refs[:6]
    blocks = refs[6 : 6 + group]
    mods = refs[6 + group : 6 + 2 * group]
    outs = refs[6 + 2 * group :]
    (probs_ref, picked_ref, gathered_ref, x0_ref, n1_ref) = outs[:5]
    units = outs[5 : 5 + CUTS]
    qkv_w, mod_s, mask_s, unit_s = outs[5 + CUTS :]
    item = pl.program_id(0)
    grp, seq = place()
    tokens = fields_ref.shape[1]

    @pl.when(item == 0)
    def _():
        assemble(qkv_w, blocks, grp, 0, 3 * D)
        total = mods[0][...]
        for m in mods[1:]:
            total = total + m[...]
        mod_s[...] = total

    fields = fields_ref[0]
    wide_fields = fields.astype(F32)
    keep, pad = widen_mask(mask_ref, mask_s)
    scores = nt(fields, score_ref[...])
    expand = jnp.where(spread(), 1.0, 0.0).astype(BF16)
    low = half_low((tokens, 128))
    for j in range(HEADS // 2):
        pair = []
        for h in (2 * j, 2 * j + 1):
            s = jnp.where(
                keep, scores[:, h * 128 : (h + 1) * 128], jnp.where(pad, -3e38, masked_score)
            )
            e = jnp.exp(s - jnp.max(s, axis=-1, keepdims=True))
            a = e / jnp.sum(e, axis=-1, keepdims=True)
            probs_ref[0, :, h * 128 : (h + 1) * 128] = a
            picked = (nn(a.astype(BF16), expand) * wide_fields).astype(BF16)
            picked_ref[h] = picked
            pair.append(nt(picked, fused_ref[j * 128 : (j + 1) * 128, :]))
        gathered_ref[:, j * 128 : (j + 1) * 128] = jnp.where(low, pair[0], pair[1]).astype(BF16)
    x0 = nn(gathered_ref[...], agg_ref[:, 2 * D :])
    x0_ref[...] = x0
    mod = mod_s[pl.ds(interval[item], 1), :]
    normed, _ = standardize(x0)
    n1 = (normed * (1.0 + mod[:, D : 2 * D]) + mod[:, :D]).astype(BF16)
    n1_ref[...] = n1
    qkv = nn(n1, qkv_w[...])
    half = tokens // 2
    low = half_low((half, 128))
    for h in range(HEADS):
        unit_s[HEADS * item + h, :tokens, :] = qkv[:, h * 128 : (h + 1) * 128].astype(BF16)
    for j in range(HEADS // 2):
        pair = qkv[:, 2 * D + j * 128 : 2 * D + (j + 1) * 128]
        top, bottom = pair[:half], pair[half:]
        unit_s[HEADS * item + 2 * j, tokens:, :] = jnp.where(
            low, top, swap_halves(bottom)
        ).astype(BF16)
        unit_s[HEADS * item + 2 * j + 1, tokens:, :] = jnp.where(
            low, swap_halves(top), bottom
        ).astype(BF16)

    @pl.when(item == pl.num_programs(0) - 1)
    def _():
        deal(units, unit_s, seq)


def deal(targets, source, seq):
    a = seq // (lax.axis_size("seq") // CUTS)
    for m in range(CUTS):
        for r in range(targets[m].shape[0]):
            targets[m][r] = source[CUTS * r + jnp.bitwise_xor(a, m)]


def collect(target, sources, seq):
    a = seq // (lax.axis_size("seq") // CUTS)
    for m in range(CUTS):
        for r in range(sources[m].shape[0]):
            target[CUTS * r + jnp.bitwise_xor(a, m)] = sources[m][r]


def unpack(pack, at_low):
    wide = pack.astype(F32)
    low = half_low(wide.shape)
    if at_low:
        both = [jnp.where(low, wide, 0.0), jnp.where(low, swap_halves(wide), 0.0)]
    else:
        both = [jnp.where(low, 0.0, swap_halves(wide)), jnp.where(low, 0.0, wide)]
    return jnp.concatenate(both, axis=0).astype(BF16)


def pack_rows(tile, at_low):
    half = tile.shape[0] // 2
    top, bottom = tile[:half], tile[half:]
    low = half_low(top.shape)
    if at_low:
        return jnp.where(low, top, swap_halves(bottom))
    return jnp.where(low, swap_halves(top), bottom)


def attend(shares, *refs):
    own = refs[:CUTS]
    others = refs[CUTS : CUTS * shares]
    backs = refs[CUTS * shares : CUTS * shares + CUTS]
    kept_ref, lse_ref, keys_s, turned_s = refs[CUTS * shares + CUTS :]
    tokens = kept_ref.shape[2]
    for n, ref in enumerate(own + others):
        keys_s[n * tokens : (n + 1) * tokens, :] = ref[0, :tokens, :]
    keys = keys_s[...]
    turned_s[...] = keys.T
    for m in range(CUTS):
        queries = unpack(own[m][0, tokens:, :], True)
        scores = nt(keys, queries) * (SCALE * LOG2E)
        top = jnp.max(scores, axis=0, keepdims=True)
        probs = jnp.exp2(scores - top)
        total = jnp.sum(probs, axis=0, keepdims=True)
        out = nn(turned_s[...], probs.astype(BF16)) / total
        lse_ref[0, m] = jnp.broadcast_to(top + jnp.log2(total), (8, tokens))
        out = out.T
        kept_ref[0, m] = out
        backs[m][0] = pack_rows(out, False).astype(BF16)


def middle(group, *refs):
    (interval, wl, wg, x0_ref, fields_ref, mask_ref) = refs[:6]
    heads_in = refs[6 : 6 + CUTS]
    blocks = refs[6 + CUTS : 6 + CUTS + group]
    mods = refs[6 + CUTS + group : 6 + CUTS + 2 * group]
    outs = refs[6 + CUTS + 2 * group :]
    (dx1_ref, rows_ref, keep_ref, send_ref, loss_ref) = outs[:5]
    sends = outs[5 : 5 + CUTS]
    weights, mod_s, mask_s, head_s, grad_s, attended_s, acc = outs[5 + CUTS :]
    item = pl.program_id(0)
    grp, seq = place()
    tokens = x0_ref.shape[0]
    half = tokens // 2

    @pl.when(item == 0)
    def _():
        assemble(weights, blocks, grp, 0, D + FF + OUTP + FF)
        total = mods[0][...]
        for m in mods[1:]:
            total = total + m[...]
        mod_s[...] = total
        collect(head_s, heads_in, seq)
        acc[...] = jnp.zeros_like(acc)
        loss_ref[...] = jnp.zeros_like(loss_ref)

    low = half_low((half, 128))
    for j in range(HEADS // 2):
        one = head_s[HEADS * item + 2 * j].astype(F32)
        two = head_s[HEADS * item + 2 * j + 1].astype(F32)
        attended_s[:half, j * 128 : (j + 1) * 128] = jnp.where(low, one, swap_halves(two)).astype(
            BF16
        )
        attended_s[half:, j * 128 : (j + 1) * 128] = jnp.where(low, swap_halves(one), two).astype(
            BF16
        )
    out_w = slice(0, D)
    up_w = slice(D, D + FF)
    head_w = slice(D + FF, D + FF + OUT)
    down_w = slice(D + FF + OUTP, D + FF + OUTP + FF)
    mod = mod_s[pl.ds(interval[item], 1), :]
    gate_a, shift_b, scale_b, gate_b = [mod[:, k * D : (k + 1) * D] for k in range(2, 6)]
    attended = attended_s[...]
    branch_a = nn(attended, weights[:, out_w])
    x1 = x0_ref[...] + gate_a * branch_a
    normed_b, rstd_b = standardize(x1)
    n2 = (normed_b * (1.0 + scale_b) + shift_b).astype(BF16)
    value, slope = gelu_parts(nn(n2, weights[:, up_w]))
    active = value.astype(BF16)
    branch_b = nt(active, weights[:, down_w])
    x2 = x1 + gate_b * branch_b
    final, rstd_f = standardize(x2)
    nf = final.astype(BF16)
    diff = nn(nf, weights[:, head_w]) - fields_ref[0].astype(F32)
    keep, _ = widen_mask(mask_ref, mask_s)
    expand = jnp.where(spread(), 1.0, 0.0).astype(BF16)
    present = nn(jnp.where(keep, 1.0, 0.0).astype(BF16), expand)
    row = iota((tokens, 1), 0) // COLS
    weight = jnp.zeros((tokens, 1), F32)
    weight_grad = jnp.zeros((tokens, 1), F32)
    for r in range(tokens // COLS):
        weight = jnp.where(row == r, wl[item, r], weight)
        weight_grad = jnp.where(row == r, wg[item, r], weight_grad)
    masked = present * diff
    each = jnp.sum(masked * diff, axis=1, keepdims=True) * weight
    loss_ref[...] += jnp.broadcast_to(jnp.sum(each, axis=0, keepdims=True) / PIX, (8, 128))
    dpred = (masked * weight_grad).astype(BF16)

    acc[:, head_w] += tn(nf, dpred)
    dx2 = standardize_back(nt(dpred, weights[:, head_w]), final, rstd_f)
    db2 = (gate_b * dx2).astype(BF16)
    d_gate_b = jnp.sum(dx2 * branch_b, axis=0, keepdims=True)
    acc[:, down_w] += tn(db2, active)
    dh = (nn(db2, weights[:, down_w]) * slope).astype(BF16)
    acc[:, up_w] += tn(n2, dh)
    dn2 = nt(dh, weights[:, up_w])
    d_shift_b = jnp.sum(dn2, axis=0, keepdims=True)
    d_scale_b = jnp.sum(dn2 * normed_b, axis=0, keepdims=True)
    dx1 = dx2 + standardize_back(dn2 * (1.0 + scale_b), normed_b, rstd_b)
    dx1_ref[...] = dx1
    d_gate_a = jnp.sum(dx1 * branch_a, axis=0, keepdims=True)
    db1 = (gate_a * dx1).astype(BF16)
    acc[:, out_w] += tn(attended, db1)
    dout = nt(db1, weights[:, out_w])
    rows_ref[0] = jnp.concatenate(
        [d_gate_a, d_shift_b, d_scale_b, d_gate_b, jnp.zeros((4, D), F32)], axis=0
    )
    for j in range(HEADS // 2):
        pair = dout[:, j * 128 : (j + 1) * 128]
        top, bottom = pair[:half], pair[half:]
        grad_s[HEADS * item + 2 * j] = jnp.where(low, top, swap_halves(bottom)).astype(BF16)
        grad_s[HEADS * item + 2 * j + 1] = jnp.where(low, swap_halves(top), bottom).astype(BF16)

    @pl.when(item == pl.num_programs(0) - 1)
    def _():
        deal(sends, grad_s, seq)
        split_rows(acc, grp, keep_ref, send_ref)


def split_rows(acc, grp, keep_ref, send_ref):
    rows = keep_ref.shape[1]
    for j in range(keep_ref.shape[0]):
        for odd, ref in ((0, keep_ref), (1, send_ref)):
            at = pl.multiple_of(jnp.bitwise_xor(grp, 2 * j + odd) * rows, 16)
            ref[j] = acc[pl.ds(at, rows), :].astype(BF16)


def attend_back(shares, *refs):
    own = refs[:CUTS]
    others = refs[CUTS : CUTS * shares]
    grads = refs[CUTS * shares : CUTS * shares + CUTS]
    kept_ref, lse_ref = refs[CUTS * shares + CUTS : CUTS * shares + CUTS + 2]
    outs = refs[CUTS * shares + CUTS + 2 :]
    dq_ref, own_ref = outs[:2]
    far_refs = outs[2 : 2 + shares - 1]
    keys_s, turned_s, acc = outs[2 + shares - 1 :]
    tokens = kept_ref.shape[2]
    for n, ref in enumerate(own + others):
        keys_s[n * tokens : (n + 1) * tokens, :] = ref[0, :tokens, :]
    keys = keys_s[...]
    turned_s[...] = keys.T
    for m in range(CUTS):
        queries = unpack(own[m][0, tokens:, :], True)
        grad = unpack(grads[m][0], False)
        delta = jnp.sum((grad.astype(F32) * kept_ref[0, m]).T, axis=0, keepdims=True)
        scores = nt(keys, queries) * (SCALE * LOG2E)
        probs = jnp.exp2(scores - lse_ref[0, m, 0:1, :])
        dprobs = nt(keys, grad)
        dscores = (probs * (dprobs - delta)).astype(BF16)
        step = nn(probs.astype(BF16), grad) + nn(dscores, queries)
        if m == 0:
            acc[...] = step
        else:
            acc[...] += step
        dq = nn(turned_s[...], dscores).T * SCALE
        dq_ref[0, m] = pack_rows(dq, True).astype(BF16)
    factor = jnp.where(half_low((1, 128)), SCALE, 1.0)
    for m in range(CUTS):
        own_ref[0, m] = (acc[m * tokens : (m + 1) * tokens, :] * factor).astype(BF16)
        for n, ref in enumerate(far_refs):
            at = ((n + 1) * CUTS + m) * tokens
            ref[0, m] = (acc[at : at + tokens, :] * factor).astype(BF16)


def join_back(shares, *refs):
    dq_ref, own_ref = refs[:2]
    far = refs[2 : 2 + shares - 1]
    outs = refs[2 + shares - 1 :]
    tokens = own_ref.shape[2]
    for m in range(CUTS):
        for r in range(own_ref.shape[0]):
            total = own_ref[r, m].astype(F32)
            for ref in far:
                total = total + ref[r, m].astype(F32)
            outs[m][r, :tokens, :] = total.astype(BF16)
            outs[m][r, tokens:, :] = dq_ref[r, m]


def early_back(group, *refs):
    (interval, x0_ref, n1_ref, dx1_ref, rows_ref, gathered_ref, probs_ref, picked_ref) = refs[:8]
    (fields_ref, mask_ref, fused_ref, agg_ref, embed_ref, probe_ref) = refs[8:14]
    units = refs[14 : 14 + CUTS]
    blocks = refs[14 + CUTS : 14 + CUTS + group]
    mods = refs[14 + CUTS + group : 14 + CUTS + 2 * group]
    outs = refs[14 + CUTS + 2 * group :]
    (keep_ref, send_ref, dmod_ref) = outs[:3]
    qkv_w, mod_s, mask_s, unit_s, dqkv_s, acc, mix, dscore = outs[3:]
    item = pl.program_id(0)
    grp, seq = place()
    tokens = x0_ref.shape[0]
    half = tokens // 2
    qkv_at = 3 * D + OUTP

    @pl.when(item == 0)
    def _():
        assemble(qkv_w, blocks, grp, 0, 3 * D)
        total = mods[0][...]
        for m in mods[1:]:
            total = total + m[...]
        mod_s[...] = total
        collect(unit_s, units, seq)
        acc[...] = jnp.zeros_like(acc)
        mix[...] = jnp.zeros_like(mix)
        dscore[...] = jnp.zeros_like(dscore)
        dmod_ref[...] = jnp.zeros_like(dmod_ref)

    low = half_low((half, 128))
    for h in range(HEADS):
        dqkv_s[:, h * 128 : (h + 1) * 128] = unit_s[HEADS * item + h, :tokens, :]
    for j in range(HEADS // 2):
        one = unit_s[HEADS * item + 2 * j, tokens:, :].astype(F32)
        two = unit_s[HEADS * item + 2 * j + 1, tokens:, :].astype(F32)
        lanes = slice(2 * D + j * 128, 2 * D + (j + 1) * 128)
        dqkv_s[:half, lanes] = jnp.where(low, one, swap_halves(two)).astype(BF16)
        dqkv_s[half:, lanes] = jnp.where(low, swap_halves(one), two).astype(BF16)
    dqkv = dqkv_s[...]
    which = interval[item]
    mod = mod_s[pl.ds(which, 1), :]
    acc[:, qkv_at:] += tn(n1_ref[...], dqkv)
    dn1 = nt(dqkv, qkv_w[...])
    normed, rstd = standardize(x0_ref[...])
    d_shift = jnp.sum(dn1, axis=0, keepdims=True)
    d_scale = jnp.sum(dn1 * normed, axis=0, keepdims=True)
    dx0 = (
        dx1_ref[...] + standardize_back(dn1 * (1.0 + mod[:, D : 2 * D]), normed, rstd)
    ).astype(BF16)
    rows = rows_ref[0]
    for k, row in enumerate([d_shift, d_scale] + [rows[r : r + 1] for r in range(4)]):
        dmod_ref[pl.ds(which, 1), k * D : (k + 1) * D] += row

    acc[:, 2 * D : 3 * D] += tn(gathered_ref[...], dx0)
    dagg = nt(dx0, agg_ref[:, 2 * D :])
    fields = fields_ref[0]
    wide_fields = fields.astype(F32)
    keep, _ = widen_mask(mask_ref, mask_s)
    expand = jnp.where(spread(), 1.0, 0.0).astype(BF16)
    lower = half_low((tokens, 128))
    for j in range(HEADS // 2):
        pair = slice(j * 128, (j + 1) * 128)
        for h in (2 * j, 2 * j + 1):
            mine = lower if h % 2 == 0 else jnp.logical_not(lower)
            dpart = jnp.where(mine, dagg[:, pair], 0.0).astype(BF16)
            mix[pair, :] += tn(dpart, picked_ref[h])
            spreaded = (nn(dpart, fused_ref[pair, :]) * wide_fields).astype(BF16)
            dprobs = nt(spreaded, expand)
            probs = probs_ref[0, :, h * 128 : (h + 1) * 128]
            ds = probs * (dprobs - jnp.sum(probs * dprobs, axis=-1, keepdims=True))
            ds = jnp.where(keep, ds, 0.0).astype(BF16)
            dscore[h] += tn(ds, fields)

    @pl.when(item == pl.num_programs(0) - 1)
    def _():
        lines = iota((128, OUT), 0)
        owned = spread()
        drows = jnp.zeros((128, OUT), F32)
        for h in range(HEADS):
            line = jnp.sum(jnp.where(owned, dscore[h], 0.0), axis=0, keepdims=True) * SCALE
            drows = drows + jnp.where(lines == h, line, 0.0)
        drows = drows.astype(BF16)
        mixed = mix[...].astype(BF16)
        embed = embed_ref[:, :OUT]
        acc[:, 3 * D : 3 * D + OUT] = nn(agg_ref[:, D : 2 * D], mixed) + nn(probe_ref[...], drows)
        acc[:, D : 2 * D] = nt(embed, mixed)
        dprobe = nt(embed, drows)
        heads = jnp.where(iota((128, D), 1) // HEAD == iota((128, D), 0), 1.0, 0.0).astype(BF16)
        coarse = dprobe.astype(BF16)
        fine = (dprobe - coarse.astype(F32)).astype(BF16)
        by_column = nn(coarse, heads) + nn(fine, heads)
        eye = iota((D, D), 0) == iota((D, D), 1)
        query = embed_ref[:, OUT : OUT + 1].astype(F32)
        query_row = jnp.sum(jnp.where(eye, query, 0.0), axis=0, keepdims=True)
        acc[:, :D] = by_column * query_row
        dquery = jnp.sum(agg_ref[:, :D].astype(F32) * by_column, axis=0, keepdims=True)
        column = jnp.sum(jnp.where(eye, dquery, 0.0), axis=1, keepdims=True)
        acc[:, 3 * D + OUT : 3 * D + OUTP] = jnp.where(
            iota((D, OUTP - OUT), 1) == 0, column, 0.0
        )
        split_rows(acc, grp, keep_ref, send_ref)


def sum_cores(keep_ref, got_ref, *outs):
    for j, ref in enumerate(outs):
        ref[...] = (keep_ref[j].astype(F32) + got_ref[j].astype(F32)).astype(BF16)


def cut_granules(parts, *refs):
    sources, outs, table = refs[: -parts - 1], refs[-parts - 1 : -1], refs[-1]
    _, seq = place()
    total = sources[0][...].astype(F32)
    for ref in sources[1:]:
        total = total + ref[...].astype(F32)
    total = total.astype(BF16)
    rows, cols = total.shape
    per = rows // 16
    if table.shape[0] > per * (cols // 128):
        table[...] = jnp.zeros_like(table)
    for t in range(cols // 128):
        for g in range(per):
            table[t * per + g] = total[g * 16 : (g + 1) * 16, t * 128 : (t + 1) * 128]
    size = outs[0].shape[0]
    for j in range(parts):
        outs[j][...] = table[pl.ds(jnp.bitwise_xor(seq, j) * size, size)]


def sum_pieces(*refs):
    sources, (out_ref, square_ref) = refs[:-2], refs[-2:]
    total = sources[0][...].astype(F32)
    for ref in sources[1:]:
        total = total + ref[...].astype(F32)
    out_ref[...] = total.astype(BF16)
    square_ref[...] = jnp.sum(total * total, axis=0)


def all_squares(copies, early_ref, late_ref, loss_ref, lead_ref, dmod_ref, out_ref, dmod_out):
    grp, _ = place()
    rows = dmod_out.shape[0]
    lead = lead_ref[pl.ds(pl.multiple_of(grp * rows, 16), rows), :].astype(F32)
    grad = lead[:, 0:1] * dmod_ref[0:1, :]
    for g in (1, 2):
        grad = grad + lead[:, g : g + 1] * dmod_ref[g : g + 1, :]
    dmod_out[...] = grad
    squares = jnp.sum(early_ref[...] + late_ref[...]) + jnp.sum(grad * grad) / copies
    which = iota((8, 128), 0)
    out_ref[...] = jnp.where(which == 0, loss_ref[...], squares)


def step_values(param, first, second, grad):
    first = beta_first * first + (1.0 - beta_first) * grad
    second = beta_second * second + (1.0 - beta_second) * grad * grad
    mean_hat = first / (1.0 - beta_first**STEP)
    var_hat = second / (1.0 - beta_second**STEP)
    param = param - learn_rate * (
        mean_hat / (jnp.sqrt(var_hat) + adam_epsilon) + decay_rate * param
    )
    return param, first, second, param.astype(BF16)


def optimize(parts, *refs):
    reduced_ref = refs[0]
    early = refs[1 : 1 + parts]
    late = refs[1 + parts : 1 + 2 * parts]
    dmod_ref = refs[1 + 2 * parts]
    wide = refs[2 + 2 * parts : 5 + 2 * parts]
    tall = refs[5 + 2 * parts : 8 + 2 * parts]
    query = refs[8 + 2 * parts : 11 + 2 * parts]
    outs = refs[11 + 2 * parts :]
    norm_ref, wide_out, tall_out, query_out = outs[0], outs[1:5], outs[5:9], outs[9:13]
    early_s, late_s = outs[13:]
    _, seq = place()
    for table, pieces in ((early_s, early), (late_s, late)):
        size = pieces[0].shape[0]
        for j, ref in enumerate(pieces):
            table[pl.ds(jnp.bitwise_xor(seq, j) * size, size)] = ref[...]
    norm = jnp.sqrt(reduced_ref[1:2, 0:1])
    norm_ref[...] = jnp.broadcast_to(norm, norm_ref.shape)
    factor = jnp.minimum(1.0, clip_limit / (norm + 1e-06))
    rows = wide[0].shape[0]
    per = rows // 16

    def tile(table, t):
        return jnp.concatenate(
            [table[t * per + g] for g in range(per)], axis=0
        ).astype(F32)

    def put(ins, targets, at, grad):
        new = step_values(*[r[at] for r in ins], grad * factor)
        for ref, value in zip(targets, new):
            ref[at] = value

    def wide_at(t, width=128):
        return (slice(None), slice(t * 128, t * 128 + width))

    low = half_low((rows, 128))
    for t in range(9):
        put(wide, wide_out, wide_at(t), tile(late_s, t))
    for t in range(18):
        put(wide, wide_out, wide_at(9 + t), dmod_ref[:, t * 128 : (t + 1) * 128])
    qkv = 18
    for j in range(3):
        put(wide, wide_out, wide_at(27 + j), tile(late_s, qkv + 6 + j))
        one, two = tile(late_s, qkv + 2 * j), tile(late_s, qkv + 2 * j + 1)
        put(wide, wide_out, wide_at(30 + j), jnp.where(low, one, swap_halves(two)))
        put(wide, wide_out, wide_at(33 + j), jnp.where(low, swap_halves(one), two))
    for t in range(15 + 8):
        put(wide, wide_out, wide_at(36 + t), tile(early_s, t))
    rest = OUT - 8 * 128
    put(wide, wide_out, wide_at(59, rest), tile(early_s, 23)[:, :rest])
    for t in range(9):
        grad = tile(late_s, 9 + t).T
        if t < 8:
            put(tall, tall_out, (slice(t * 128, (t + 1) * 128), slice(None)), grad)
        else:
            put(tall, tall_out, (slice(t * 128, OUT), slice(None)), grad[:rest])
            put(query, query_out, (slice(None), slice(None)), grad[rest : rest + 1])
    for t in range(FF // 128):
        at = OUT + t * 128
        put(tall, tall_out, (slice(at, at + 128), slice(None)), tile(early_s, 24 + t).T)


def shift(value, axis, bit):
    size = lax.axis_size(axis)
    return lax.ppermute(value, axis, [(i, i ^ bit) for i in range(size)])


def gather_blocks(own, group):
    blocks = {0: own}
    for j in range(2, group, 2):
        blocks[j] = shift(own, "grp", j)
    for j in range(0, group, 2):
        blocks[j + 1] = shift(blocks[j], "grp", 1)
    return [blocks[j] for j in range(group)]


def reduce_granules(keep, send, group, parts):
    _, rows, cols = keep.shape
    got = shift(send, "grp", 1)
    halves = call(sum_cores, [sds((rows, cols), BF16)] * (group // 2))(keep, got)
    sums = [halves[0]] + [shift(halves[j], "grp", 2 * j) for j in range(1, group // 2)]
    count = (rows // 16) * (cols // 128)
    size = -(-count // parts)
    pieces = call(
        functools.partial(cut_granules, parts),
        [sds((size, 16, 128), BF16)] * parts,
        scratch=[pltpu.VMEM((size * parts, 16, 128), BF16)],
    )(*sums)
    pieces = [pieces[0]] + [shift(pieces[j], "seq", j) for j in range(1, parts)]
    return call(sum_pieces, [sds((size, 16, 128), BF16), sds((16, 128), F32)])(*pieces)


def gather_pieces(piece, parts):
    return [piece] + [shift(piece, "seq", j) for j in range(1, parts)]


def butterfly(value, axes):
    for axis in axes:
        bit = 1
        while bit < lax.axis_size(axis):
            value = value + shift(value, axis, bit)
            bit *= 2
    return value


def lead_features(interval, width):
    hours = 6.0 * jnp.exp2(interval.astype(F32))
    half = width // 2
    freqs = jnp.exp(-jnp.log(1000.0) * jnp.arange(half, dtype=F32) / half)
    angles = hours[:, None] * freqs[None, :]
    return jax.nn.silu(jnp.concatenate([jnp.sin(angles), jnp.cos(angles)], axis=-1))


def per_device(
    fields,
    targets,
    land_mask,
    interval,
    samples,
    wide_weights,
    wide_firsts,
    wide_seconds,
    tall_weights,
    tall_firsts,
    tall_seconds,
    query_vector,
    query_firsts,
    query_seconds,
):
    group = lax.axis_size("grp")
    parts = lax.axis_size("seq")
    shares = parts // CUTS
    rows, columns = wide_weights.shape
    items, tokens = fields.shape[:2]
    units = items * HEADS // CUTS
    every = items * tokens
    late_cols = D + FF + OUTP + FF

    query_row = query_vector.reshape(1, rows)
    lead = lead_features(jnp.arange(3, dtype=jnp.int32), D).astype(BF16)
    lead_columns = jnp.zeros((D, 128), BF16).at[:, :3].set(lead.T)

    first_own = call(
        pack_first,
        sds((rows, 3 * D + OUTP), BF16),
        grid=(1,),
        in_specs=[
            pl.BlockSpec((rows, 3 * D), lambda i: (0, 0)),
            pl.BlockSpec((OUT, rows), lambda i: (0, 0)),
            pl.BlockSpec((1, rows), lambda i: (0, 0)),
        ],
        out_specs=pl.BlockSpec((rows, 3 * D + OUTP), lambda i: (0, 0)),
    )(wide_weights, tall_weights, query_row)
    first = gather_blocks(first_own, group)
    qkv_own, late_own, mod_own = call(
        pack_rest,
        [
            sds((rows, 3 * D), BF16),
            sds((rows, late_cols), BF16),
            sds((8, 6 * D), F32),
        ],
    )(wide_weights, tall_weights, lead_columns)
    qkv_blocks = gather_blocks(qkv_own, group)
    mods = gather_blocks(mod_own, group)
    late_blocks = gather_blocks(late_own, group)

    lines = tokens // COLS
    line = lax.axis_index("seq") * lines + jnp.arange(lines)
    latitude = jnp.pi * ((line.astype(F32) + 0.5) / (lines * parts) - 0.5)
    weight_lines = samples.astype(F32)[:, None] * jnp.cos(latitude)[None, :]
    present = jnp.sum(land_mask.reshape(items, lines, COLS * VARS), axis=-1).astype(F32)
    weight_sum = butterfly(
        jnp.broadcast_to(jnp.sum(weight_lines * present), (8, 128)), ("grp", "seq")
    )[0, 0]
    weight_grads = weight_lines * (2.0 / PIX) / weight_sum

    agg_weights, embed, score_w, fused_w, probe = call(
        prepare,
        [
            sds((D, 3 * D), BF16),
            sds((D, OUTP), BF16),
            sds((HEADS * 128, OUT), BF16),
            sds((D, OUT), BF16),
            sds((D, 128), BF16),
        ],
    )(*first)

    by_item = pl.BlockSpec((tokens, D), lambda i: (i, 0))

    def item_block(width):
        return pl.BlockSpec((1, tokens, width), lambda i: (i, 0, 0))

    heads_spec = pl.BlockSpec((HEADS, tokens, OUT), lambda i: (0, i, 0))
    packed = tokens + tokens // 2

    results = call(
        functools.partial(aggregate, group),
        [
            sds((items, tokens, HEADS * 128), F32),
            sds((HEADS, every, OUT), BF16),
            sds((every, D), BF16),
            sds((every, D), F32),
            sds((every, D), BF16),
        ]
        + [sds((units, packed, 128), BF16)] * CUTS,
        grid=(items,),
        in_specs=[smem(), item_block(OUT), item_block(VARS)] + [whole()] * (3 + 2 * group),
        out_specs=[item_block(HEADS * 128), heads_spec, by_item, by_item, by_item]
        + [whole()] * CUTS,
        scratch=[
            pltpu.VMEM((D, 3 * D), BF16),
            pltpu.VMEM((8, 6 * D), F32),
            pltpu.VMEM((tokens, 128), jnp.int32),
            pltpu.VMEM((items * HEADS, packed, 128), BF16),
        ],
    )(interval, fields, land_mask, score_w, fused_w, agg_weights, *qkv_blocks, *mods)
    probs, picked, gathered, x0, n1 = results[:5]
    dealt = results[5:]

    own = [dealt[0]] + [shift(dealt[m], "seq", m * shares) for m in range(1, CUTS)]
    others = [shift(own[m], "seq", n) for n in range(1, shares) for m in range(CUTS)]
    keys_total = parts * tokens

    unit_in = pl.BlockSpec((1, packed, 128), lambda u: (u, 0, 0))
    half_in = pl.BlockSpec((1, tokens // 2, 128), lambda u: (u, 0, 0))
    kept_spec = pl.BlockSpec((1, CUTS, tokens, 128), lambda u: (u, 0, 0, 0))
    lse_spec = pl.BlockSpec((1, CUTS, 8, tokens), lambda u: (u, 0, 0, 0))
    pack_spec = pl.BlockSpec((1, CUTS, tokens // 2, 128), lambda u: (u, 0, 0, 0))
    half_out = sds((units, tokens // 2, 128), BF16)
    results = call(
        functools.partial(attend, shares),
        [half_out] * CUTS
        + [sds((units, CUTS, tokens, 128), F32), sds((units, CUTS, 8, tokens), F32)],
        grid=(units,),
        in_specs=[unit_in] * (CUTS * shares),
        out_specs=[half_in] * CUTS + [kept_spec, lse_spec],
        scratch=[pltpu.VMEM((keys_total, 128), BF16), pltpu.VMEM((128, keys_total), BF16)],
    )(*own, *others)
    backs, kept, lse = results[:CUTS], results[CUTS], results[CUTS + 1]
    heads_in = [backs[0]] + [shift(backs[m], "seq", m * shares) for m in range(1, CUTS)]

    results = call(
        functools.partial(middle, group),
        [
            sds((every, D), F32),
            sds((items, 8, D), F32),
            sds((group // 2, rows, late_cols), BF16),
            sds((group // 2, rows, late_cols), BF16),
            sds((8, 128), F32),
        ]
        + [half_out] * CUTS,
        grid=(items,),
        in_specs=[smem(), smem(), smem(), by_item, item_block(OUT), item_block(VARS)]
        + [whole()] * (CUTS + 2 * group),
        out_specs=[by_item, pl.BlockSpec((1, 8, D), lambda i: (i, 0, 0))] + [whole()] * (3 + CUTS),
        scratch=[
            pltpu.VMEM((D, late_cols), BF16),
            pltpu.VMEM((8, 6 * D), F32),
            pltpu.VMEM((tokens, 128), jnp.int32),
            pltpu.VMEM((items * HEADS, tokens // 2, 128), BF16),
            pltpu.VMEM((items * HEADS, tokens // 2, 128), BF16),
            pltpu.VMEM((tokens, D), BF16),
            pltpu.VMEM((D, late_cols), F32),
        ],
    )(
        interval,
        weight_lines,
        weight_grads,
        x0,
        targets,
        land_mask,
        *heads_in,
        *late_blocks,
        *mods,
    )
    dx1, mod_rows, early_keep, early_send, loss = results[:5]
    sends = results[5:]
    grads_in = [sends[0]] + [shift(sends[m], "seq", m * shares) for m in range(1, CUTS)]

    early_piece, early_squares = reduce_granules(early_keep, early_send, group, parts)

    results = call(
        functools.partial(attend_back, shares),
        [sds((units, CUTS, tokens // 2, 128), BF16)]
        + [sds((units, CUTS, tokens, 128), BF16)] * shares,
        grid=(units,),
        in_specs=[unit_in] * (CUTS * shares) + [half_in] * CUTS + [kept_spec, lse_spec],
        out_specs=[pack_spec] + [kept_spec] * shares,
        scratch=[
            pltpu.VMEM((keys_total, 128), BF16),
            pltpu.VMEM((128, keys_total), BF16),
            pltpu.VMEM((keys_total, 128), F32),
        ],
    )(*own, *others, *grads_in, kept, lse)
    dq, near, far = results[0], results[1], results[2:]
    far = [shift(far[n], "seq", n + 1) for n in range(shares - 1)]
    dealt = call(
        functools.partial(join_back, shares), [sds((units, packed, 128), BF16)] * CUTS
    )(dq, near, *far)
    units_in = [dealt[0]] + [shift(dealt[m], "seq", m * shares) for m in range(1, CUTS)]

    first_cols = 3 * D + OUTP + 3 * D
    late_keep, late_send, dmod = call(
        functools.partial(early_back, group),
        [
            sds((group // 2, rows, first_cols), BF16),
            sds((group // 2, rows, first_cols), BF16),
            sds((8, 6 * D), F32),
        ],
        grid=(items,),
        in_specs=[
            smem(),
            by_item,
            by_item,
            by_item,
            pl.BlockSpec((1, 8, D), lambda i: (i, 0, 0)),
            by_item,
            item_block(HEADS * 128),
            heads_spec,
            item_block(OUT),
            item_block(VARS),
        ]
        + [whole()] * (4 + CUTS + 2 * group),
        out_specs=[whole()] * 3,
        scratch=[
            pltpu.VMEM((D, 3 * D), BF16),
            pltpu.VMEM((8, 6 * D), F32),
            pltpu.VMEM((tokens, 128), jnp.int32),
            pltpu.VMEM((items * HEADS, packed, 128), BF16),
            pltpu.VMEM((tokens, 3 * D), BF16),
            pltpu.VMEM((D, first_cols), F32),
            pltpu.VMEM((D, OUT), F32),
            pltpu.VMEM((HEADS, 128, OUT), F32),
        ],
    )(
        interval,
        x0,
        n1,
        dx1,
        mod_rows,
        gathered,
        probs,
        picked,
        fields,
        land_mask,
        fused_w,
        agg_weights,
        embed,
        probe,
        *units_in,
        *qkv_blocks,
        *mods,
    )
    late_piece, late_squares = reduce_granules(late_keep, late_send, group, parts)
    dmod = butterfly(dmod, ("grp", "seq"))
    reduced, grad_modulation = call(
        functools.partial(all_squares, parts),
        [sds((8, 128), F32), sds((rows, 6 * D), F32)],
    )(early_squares, late_squares, loss, lead_columns, dmod)
    reduced = butterfly(reduced, ("grp", "seq"))
    early_all = gather_pieces(early_piece, parts)
    late_all = gather_pieces(late_piece, parts)

    def like(x, dtype=F32):
        return sds(x.shape, dtype)

    results = call(
        functools.partial(optimize, parts),
        [sds((8, 128), F32)]
        + [like(wide_weights)] * 3
        + [like(wide_weights, BF16)]
        + [like(tall_weights)] * 3
        + [like(tall_weights, BF16)]
        + [like(query_row)] * 3
        + [like(query_row, BF16)],
        scratch=[
            pltpu.VMEM((parts * early_piece.shape[0], 16, 128), BF16),
            pltpu.VMEM((parts * late_piece.shape[0], 16, 128), BF16),
        ],
    )(
        reduced,
        *early_all,
        *late_all,
        grad_modulation,
        wide_weights,
        wide_firsts,
        wide_seconds,
        tall_weights,
        tall_firsts,
        tall_seconds,
        query_row,
        query_firsts.reshape(1, rows),
        query_seconds.reshape(1, rows),
    )
    norm = results[0]
    query_out = tuple(r.reshape(rows) for r in results[9:13])
    return (reduced[0, 0], weight_sum, norm[0, 0]) + tuple(results[1:9]) + query_out


def solution(mesh):
    placed = (
        P("grp", "seq", None),
        P("grp", "seq", None),
        P("grp", "seq", None),
        P("grp"),
        P("grp"),
        P("grp", None),
        P("grp", None),
        P("grp", None),
        P(None, "grp"),
        P(None, "grp"),
        P(None, "grp"),
        P("grp"),
        P("grp"),
        P("grp"),
    )
    return jax.shard_map(
        per_device,
        mesh=mesh,
        in_specs=placed,
        out_specs=(
            P(),
            P(),
            P(),
            P("grp", None),
            P("grp", None),
            P("grp", None),
            P("grp", None),
            P(None, "grp"),
            P(None, "grp"),
            P(None, "grp"),
            P(None, "grp"),
            P("grp"),
            P("grp"),
            P("grp"),
            P("grp"),
        ),
        check_vma=False,
    )
```

time: 836 us -> 436 us (0.52)
  matrix products: 260 us -> 0 us
  blocking collectives: 147 us -> 0 us
  starting transfers between devices: 0.37 us -> 115 us
  Pallas kernels: 0 us -> 114 us
  local copies, waits for them, and re-layouts: 110 us -> 29.8 us
  waiting for transfers between devices: 233 us -> 163 us
  other arithmetic: 54.1 us -> 4.67 us
  between operations: 20.2 us -> 1.54 us
    dot_general x40 -> x0, matrix products: 260 us -> none  [the longest x36 255 us: product(): return jnp.einsum(spec, left, right, preferred_element_type=jnp.float32)]
    ppermute x0 -> x76, waiting for transfers between devices: none -> 163 us  [shift(): return lax.ppermute(value, axis, [(i, i ^ bit) for i in range(size)])]
    ppermute x0 -> x76, starting transfers between devices: none -> 115 us  [shift(): return lax.ppermute(value, axis, [(i, i ^ bit) for i in range(size)])]
    pallas_call x0 -> x17, Pallas kernels: none -> 114 us  [the longest x1 23.3 us: per_device(): call(functools.partial(early_back, group), [sds((group // 2, rows, first_...]
    all_gather x6 -> x0, waiting for transfers between devices: 105 us -> none  [the longest x1 59.5 us: per_device(): lax.all_gather(key_low, 'seq', axis=1, tiled=True)]
    psum x1 -> x0, waiting for transfers between devices: 73.3 us -> none  [per_device(): lax.psum(wide_grad.astype(jnp.bfloat16), 'seq').astype(jnp.float32)]
    psum x3 -> x0, blocking collectives: 71 us -> none  [the longest x1 41 us: per_device(): lax.psum((loss_part, jnp.sum(weight)), ('grp', 'seq'))]
    all_gather x2 -> x0, blocking collectives: 62 us -> none  [the longest x1 31.5 us: per_device(): lax.all_gather(delta.transpose(0, 2, 1), 'seq', axis=1, tiled=True)]
  transfers between devices with their start and end apart: 9 -> 76, of which waited for: 5 -> 29; matrix products, arithmetic and copies ran while one was open for 27% -> 4% of each run, Pallas kernels for 0% -> 15%
where the time goes in v1:
time: 436 us; the launch traced here: 428 us
  waiting for transfers between devices  163 us (37%)
  starting transfers between devices  115 us (26%)
  Pallas kernels  114 us (26%)
  local copies, waits for them, and re-layouts  29.8 us (7%)
  other arithmetic  4.67 us (1%)
    ppermute x76, waiting for transfers between devices, shift(): return lax.ppermute(value, axis, [(i, i ^ bit) for i in range(size)])  163 us
    ppermute x76, starting transfers between devices, shift(): return lax.ppermute(value, axis, [(i, i ^ bit) for i in range(size)])  115 us
    unnamed x98, local copies, waits for them, and re-layouts  27.1 us
    pallas_call x1, Pallas kernels, per_device(): call(functools.partial(early_back, group), [sds((group // 2, rows, first_...  23.3 us
    pallas_call x1, Pallas kernels, per_device(): call(functools.partial(attend_back, shares), [sds((units, CUTS, tokens //...  20.5 us
    pallas_call x1, Pallas kernels, per_device(): call(functools.partial(attend, shares), [half_out] * CUTS + [sds((units,...  16.8 us
    pallas_call x1, Pallas kernels, per_device(): call(functools.partial(middle, group), [sds((every, D), F32), sds((items,...  15.8 us
    pallas_call x1, Pallas kernels, per_device(): call(functools.partial(optimize, parts), [sds((8, 128), F32)] + [like(wid...  12.6 us
  transfers between devices with their start and end apart: 76, of which 29 were waited for; matrix products, arithmetic and copies ran while one was open for 4% of the time, Pallas kernels for 15%

profile of v1, /device:TPU:0, one launch (start us, length us, event | category | flops | bytes accessed | tf_op | source)
XLA Modules:
  0.0 427.8 jit_solution(17468353657406692945)
XLA Ops:
  13.8 4.3 %collective-permute-done.6.refs_2_ = bf16[96,2304]{1,0:T(8,128)(2,1)} collective-permute-done((bf16[96,2304]{1,0:T(8,128)(2,1)S(1)}, bf16[96,2304]{1,0:T(8,128)(2,1)}, u32[]{:S(2)}, u32[]{:S(2)}) %collective-permute-start.6) | collective-permute-done | bytes 442400 | tf_op jit(solution)/shard_map/ppermute | solution.py:698
  20.2 22.3 %collective-permute-done.12.refs_12_.refs_16_.refs_24_ = f32[8,2304]{1,0:T(8,128)S(1)} collective-permute-done((f32[8,2304]{1,0:T(8,128)S(1)}, f32[8,2304]{1,0:T(8,128)S(1)}, u32[]{:S(2)}, u32[]{:S(2)}) %collective-permute-start.12) | collective-permute-done | bytes 73760 | tf_op jit(solution)/shard_map/ppermute | solution.py:698
  50.6 3.9 shard_map.254
  57.1 12.5 %shard_map.256 = (f32[2,256,768]{2,1,0:T(8,128)}, bf16[6,512,1104]{2,1,0:T(8,128)(2,1)}, bf16[512,384]{1,0:T(8,128)(2,1)S(1)}, f32[512,384]{1,0:T(8,128)}, bf16[...) custom-call(s32[2]{0:T(128)S(1)} %copy-done.34, ...), custom_call_target="tpu_custom_call" | custom-call | tf_op jit(solution)/shard_map/pallas_call | solution.py:829
  88.7 9.5 %collective-permute-done.4 = f32[8,128]{1,0:T(8,128)S(1)} collective-permute-done((f32[8,128]{1,0:T(8,128)S(1)}, f32[8,128]{1,0:T(8,128)S(1)}, u32[]{:S(2)}, u32[]{:S(2)}) %collective-permute-start.4) | collective-permute-done | bytes 4128 | tf_op jit(solution)/shard_map/ppermute | solution.py:698
  101.2 6.6 %collective-permute-done.15.refs_2_ = bf16[3,384,128]{2,1,0:T(8,128)(2,1)S(1)} collective-permute-done((bf16[3,384,128]{2,1,0:T(8,128)(2,1)S(1)}, bf16[3,384,128]{2,1,0:T(8,128)(2,1)S(1)}, u32[]{:S(2)}, u32[]{:S(2)}) %collective-permute-start.15) | collective-permute-done | bytes 294944 | tf_op jit(solution)/shard_map/ppermute | solution.py:698
  117.6 6.3 %collective-permute-done.19.refs_6_ = bf16[3,384,128]{2,1,0:T(8,128)(2,1)S(1)} collective-permute-done((bf16[3,384,128]{2,1,0:T(8,128)(2,1)S(1)}, bf16[3,384,128]{2,1,0:T(8,128)(2,1)S(1)}, u32[]{:S(2)}, u32[]{:S(2)}) %collective-permute-start.19) | collective-permute-done | bytes 294944 | tf_op jit(solution)/shard_map/ppermute | solution.py:698
  124.0 5.2 %collective-permute-done.20.refs_7_ = bf16[3,384,128]{2,1,0:T(8,128)(2,1)S(1)} collective-permute-done((bf16[3,384,128]{2,1,0:T(8,128)(2,1)S(1)}, bf16[3,384,128]{2,1,0:T(8,128)(2,1)S(1)}, u32[]{:S(2)}, u32[]{:S(2)}) %collective-permute-start.20) | collective-permute-done | bytes 294944 | tf_op jit(solution)/shard_map/ppermute | solution.py:698
  129.1 16.8 %shard_map.257 = (bf16[3,128,128]{2,1,0:T(8,128)(2,1)S(1)}, bf16[3,128,128]{2,1,0:T(8,128)(2,1)S(1)}, bf16[3,128,128]{2,1,0:T(8,128)(2,1)S(1)}, bf16[3,128,128]{...) custom-call(bf16[3,384,128]{2,1,0:T(8,128)(2,1)S(1)} %get-tuple-element.114.refs_0_, ...), custom_call_target="tpu_custom_call" | custom-call | tf_op jit(solution)/shard_map/pallas_call | solution.py:863
  146.5 3.8 collective-permute-start.23
  151.1 5.0 %collective-permute-done.22.refs_8_ = bf16[3,128,128]{2,1,0:T(8,128)(2,1)S(1)} collective-permute-done((bf16[3,128,128]{2,1,0:T(8,128)(2,1)S(1)}, bf16[3,128,128]{2,1,0:T(8,128)(2,1)S(1)}, u32[]{:S(2)}, u32[]{:S(2)}) %collective-permute-start.22) | collective-permute-done | bytes 98336 | tf_op jit(solution)/shard_map/ppermute | solution.py:698
  156.1 15.8 %shard_map.258 = (f32[512,384]{1,0:T(8,128)S(1)}, f32[2,8,384]{2,1,0:T(8,128)S(1)}, bf16[2,96,4608]{2,1,0:T(8,128)(2,1)}, bf16[2,96,4608]{2,1,0:T(8,128)(2,1)}, ...) custom-call(s32[2]{0:T(128)S(1)} %copy-done.34, ...), custom_call_target="tpu_custom_call" | custom-call | tf_op jit(solution)/shard_map/pallas_call | solution.py:875
  177.0 6.2 %collective-permute-done.37.refs_10_ = bf16[3,128,128]{2,1,0:T(8,128)(2,1)S(1)} collective-permute-done((bf16[3,128,128]{2,1,0:T(8,128)(2,1)S(1)}, bf16[3,128,128]{2,1,0:T(8,128)(2,1)S(1)}, u32[]{:S(2)}, u32[]{:S(2)}) %collective-permute-start.37) | collective-permute-done | bytes 98336 | tf_op jit(solution)/shard_map/ppermute | solution.py:698
  183.2 20.5 %shard_map.262 = (bf16[3,4,128,128]{3,2,1,0:T(8,128)(2,1)S(1)}, bf16[3,4,256,128]{3,2,1,0:T(8,128)(2,1)S(1)}, bf16[3,4,256,128]{3,2,1,0:T(8,128)(2,1)}) custom-call(bf16[3,384,128]{2,1,0:T(8,128)(2,1)S(1)} %get-tuple-element.114.refs_0_, bf16[3,384,128]{2,1,0:T(8,128)(2,1)S(1)} %collective-permute-done.14.refs_1_, ...), custom_call_target="tpu_custom_call" | custom-call | tf_op jit(solution)/shard_map/pallas_call | solution.py:915
  205.4 16.3 %collective-permute-done.39.refs_2_ = bf16[3,4,256,128]{3,2,1,0:T(8,128)(2,1)S(1)} collective-permute-done((bf16[3,4,256,128]{3,2,1,0:T(8,128)(2,1)}, bf16[3,4,256,128]{3,2,1,0:T(8,128)(2,1)S(1)}, u32[]{:S(2)}, u32[]{:S(2)}) %collective-permute-start.39) | collective-permute-done | bytes 786464 | tf_op jit(solution)/shard_map/ppermute | solution.py:698
  227.1 8.0 %collective-permute-done.40.refs_15_ = bf16[3,384,128]{2,1,0:T(8,128)(2,1)S(1)} collective-permute-done((bf16[3,384,128]{2,1,0:T(8,128)(2,1)S(1)}, bf16[3,384,128]{2,1,0:T(8,128)(2,1)S(1)}, u32[]{:S(2)}, u32[]{:S(2)}) %collective-permute-start.40) | collective-permute-done | bytes 294944 | tf_op jit(solution)/shard_map/ppermute | solution.py:698
  235.0 11.9 %collective-permute-done.41.refs_16_ = bf16[3,384,128]{2,1,0:T(8,128)(2,1)S(1)} collective-permute-done((bf16[3,384,128]{2,1,0:T(8,128)(2,1)S(1)}, bf16[3,384,128]{2,1,0:T(8,128)(2,1)S(1)}, u32[]{:S(2)}, u32[]{:S(2)}) %collective-permute-start.41) | collective-permute-done | bytes 294944 | tf_op jit(solution)/shard_map/ppermute | solution.py:698
  247.1 23.3 %shard_map.264 = (bf16[2,96,3456]{2,1,0:T(8,128)(2,1)}, bf16[2,96,3456]{2,1,0:T(8,128)(2,1)}, f32[8,2304]{1,0:T(8,128)S(1)}) custom-call(s32[2]{0:T(128)S(1)} %copy-done.34, f32[512,384]{1,0:T(8,128)} %get-tuple-element.113.refs_3_.refs_1_, bf16[512,384]{1,0:T(8,128)(2,1)S(1)} %copy-done.31, f32[512,384]{1,0:T(8,128)} %copy-done.16, ...), custom_call_target="tpu_custom_call" | custom-call | tf_op jit(solution)/shard_map/pallas_call | solution.py:936
  278.9 32.6 %collective-permute-done.53 = f32[8,2304]{1,0:T(8,128)S(1)} collective-permute-done((f32[8,2304]{1,0:T(8,128)S(1)}, f32[8,2304]{1,0:T(8,128)S(1)}, u32[]{:S(2)}, u32[]{:S(2)}) %collective-permute-start.53) | collective-permute-done | bytes 73760 | tf_op jit(solution)/shard_map/ppermute | solution.py:698
  316.0 5.0 %collective-permute-start.55 = (f32[8,2304]{1,0:T(8,128)S(1)}, f32[8,2304]{1,0:T(8,128)S(1)}, u32[]{:S(2)}, u32[]{:S(2)}) collective-permute-start(f32[8,2304]{1,0:T(8,128)S(1)} %add.86), channel_id=1, source_target_pairs={{0,2},{1,3},{2,0},{3,1},{4,6},{5,7},{6,4},{7,5},{8,10},{9,11},{10,... | collective-permute-start | bytes 221192 | tf_op jit(solution)/shard_map/ppermute | solution.py:698
  333.8 9.5 %collective-permute-start.34 = (bf16[27,16,128]{2,1,0:T(8,128)(2,1)S(1)}, bf16[27,16,128]{2,1,0:T(8,128)(2,1)S(1)}, u32[]{:S(2)}, u32[]{:S(2)}) collective-permute-start(bf16[27,16,128]{2,1,0:T(8,128)(2,1)S(1)} %get-tuple-element.133), channel_id=1, source_target_pairs={{0,6},{1,7},{2,4},{3,5},{4,2},{5,3},{6,0},{7,1},{8,14},{9,15},{10,... | collective-permute-start | bytes 331784 | tf_op jit(solution)/shard_map/ppermute | solution.py:698
  345.3 4.5 %collective-permute-start.47 = (bf16[21,16,128]{2,1,0:T(8,128)(2,1)S(1)}, bf16[21,16,128]{2,1,0:T(8,128)(2,1)S(1)}, u32[]{:S(2)}, u32[]{:S(2)}) collective-permute-start(bf16[21,16,128]{2,1,0:T(8,128)(2,1)S(1)} %get-tuple-element.164), channel_id=1, source_target_pairs={{0,3},{1,2},{2,1},{3,0},{4,7},{5,6},{6,5},{7,4},{8,11},{9,10},{10,... | collective-permute-start | bytes 258056 | tf_op jit(solution)/shard_map/ppermute | solution.py:698
  388.3 4.0 collective-permute-start.71
  406.5 12.6 %shard_map.269 = (f32[8,128]{1,0:T(8,128)S(1)}, f32[96,7632]{1,0:T(8,128)}, f32[96,7632]{1,0:T(8,128)}, f32[96,7632]{1,0:T(8,128)}, bf16[96,7632]{1,0:T(8,128)(2...) custom-call(f32[8,128]{1,0:T(8,128)S(1)} %add.93.refs_0_, ...), custom_call_target="tpu_custom_call" | custom-call | tf_op jit(solution)/shard_map/pallas_call | solution.py:1000
  (280 shorter events, 159.7 us)
Async XLA Ops:
  11.7 64.0 %collective-permute-start.25 = (bf16[96,4608]{1,0:T(8,128)(2,1)S(1)}, bf16[96,4608]{1,0:T(8,128)(2,1)}, u32[]{:S(2)}, u32[]{:S(2)}) collective-permute-start(bf16[96,4608]{1,0:T(8,128)(2,1)S(1)} %get-tuple-element.122.refs_10_), channel_id=1, source_target_pairs={{0,16},{8,24},{16,0},{24,8},{1,17},{9,25},{17,1},{25,9},{2,18},{10... | collective-permute-start | bytes 2654216 | tf_op jit(solution)/shard_map/ppermute | solution.py:698
  11.8 32.5 %collective-permute-start.5 = (bf16[96,2304]{1,0:T(8,128)(2,1)S(1)}, bf16[96,2304]{1,0:T(8,128)(2,1)S(1)}, u32[]{:S(2)}, u32[]{:S(2)}) collective-permute-start(bf16[96,2304]{1,0:T(8,128)(2,1)S(1)} %shard_map.253.refs_0_), channel_id=1, source_target_pairs={{0,8},{8,0},{16,24},{24,16},{1,9},{9,1},{17,25},{25,17},{2,10},{10... | collective-permute-start | bytes 1327112 | tf_op jit(solution)/shard_map/ppermute | solution.py:698
  11.9 32.1 %collective-permute-start.9 = (bf16[96,1152]{1,0:T(8,128)(2,1)S(1)}, bf16[96,1152]{1,0:T(8,128)(2,1)S(1)}, u32[]{:S(2)}, u32[]{:S(2)}) collective-permute-start(bf16[96,1152]{1,0:T(8,128)(2,1)S(1)} %get-tuple-element.111.refs_6_.refs_18_), channel_id=1, source_target_pairs={{0,16},{8,24},{16,0},{24,8},{1,17},{9,25},{17,1},{25,9},{2,18},{10... | collective-permute-start | bytes 663560 | tf_op jit(solution)/shard_map/ppermute | solution.py:698
  18.2 27.8 %collective-permute-start.7 = (bf16[96,2304]{1,0:T(8,128)(2,1)}, bf16[96,2304]{1,0:T(8,128)(2,1)}, u32[]{:S(2)}, u32[]{:S(2)}) collective-permute-start(bf16[96,2304]{1,0:T(8,128)(2,1)} %collective-permute-done.6.refs_2_), channel_id=1, source_target_pairs={{0,8},{8,0},{16,24},{24,16},{1,9},{9,1},{17,25},{25,17},{2,10},{10... | collective-permute-start | bytes 1327112 | tf_op jit(solution)/shard_map/ppermute | solution.py:698
  18.2 24.3 %collective-permute-start.12 = (f32[8,2304]{1,0:T(8,128)S(1)}, f32[8,2304]{1,0:T(8,128)S(1)}, u32[]{:S(2)}, u32[]{:S(2)}) collective-permute-start(f32[8,2304]{1,0:T(8,128)S(1)} %get-tuple-element.112.refs_10_.refs_14_.refs_22_), channel_id=1, source_target_pairs={{0,16},{8,24},{16,0},{24,8},{1,17},{9,25},{17,1},{25,9},{2,18},{10... | collective-permute-start | bytes 221192 | tf_op jit(solution)/shard_map/ppermute | solution.py:698
  46.6 26.9 %collective-permute-start = (f32[8,128]{1,0:T(8,128)S(1)}, f32[8,128]{1,0:T(8,128)S(1)}, u32[]{:S(2)}, u32[]{:S(2)}) collective-permute-start(f32[8,128]{1,0:T(8,128)S(1)} %broadcast_in_dim.2), channel_id=1, source_target_pairs={{0,8},{8,0},{16,24},{24,16},{1,9},{9,1},{17,25},{25,17},{2,10},{10... | collective-permute-start | bytes 12296 | tf_op jit(solution)/shard_map/ppermute | solution.py:698
  71.7 27.9 %collective-permute-start.14 = (bf16[3,384,128]{2,1,0:T(8,128)(2,1)S(1)}, bf16[3,384,128]{2,1,0:T(8,128)(2,1)S(1)}, u32[]{:S(2)}, u32[]{:S(2)}) collective-permute-start(bf16[3,384,128]{2,1,0:T(8,128)(2,1)S(1)} %get-tuple-element.115), channel_id=1, source_target_pairs={{0,2},{1,3},{2,0},{3,1},{4,6},{5,7},{6,4},{7,5},{8,10},{9,11},{10,... | collective-permute-start | bytes 884744 | tf_op jit(solution)/shard_map/ppermute | solution.py:698
  75.8 75.3 %collective-permute-start.24 = (bf16[96,4608]{1,0:T(8,128)(2,1)S(1)}, bf16[96,4608]{1,0:T(8,128)(2,1)}, u32[]{:S(2)}, u32[]{:S(2)}) collective-permute-start(bf16[96,4608]{1,0:T(8,128)(2,1)S(1)} %get-tuple-element.122.refs_10_), channel_id=1, source_target_pairs={{0,8},{8,0},{16,24},{24,16},{1,9},{9,1},{17,25},{25,17},{2,10},{10... | collective-permute-start | bytes 2654216 | tf_op jit(solution)/shard_map/ppermute | solution.py:698
  75.8 80.3 %collective-permute-start.26 = (bf16[96,4608]{1,0:T(8,128)(2,1)}, bf16[96,4608]{1,0:T(8,128)(2,1)}, u32[]{:S(2)}, u32[]{:S(2)}) collective-permute-start(bf16[96,4608]{1,0:T(8,128)(2,1)} %collective-permute-done.25.refs_12_), channel_id=1, source_target_pairs={{0,8},{8,0},{16,24},{24,16},{1,9},{9,1},{17,25},{25,17},{2,10},{10... | collective-permute-start | bytes 2654216 | tf_op jit(solution)/shard_map/ppermute | solution.py:698
  88.4 19.3 %collective-permute-start.15 = (bf16[3,384,128]{2,1,0:T(8,128)(2,1)S(1)}, bf16[3,384,128]{2,1,0:T(8,128)(2,1)S(1)}, u32[]{:S(2)}, u32[]{:S(2)}) collective-permute-start(bf16[3,384,128]{2,1,0:T(8,128)(2,1)S(1)} %get-tuple-element.116), channel_id=1, source_target_pairs={{0,4},{1,5},{2,6},{3,7},{4,0},{5,1},{6,2},{7,3},{8,12},{9,13},{10,... | collective-permute-start | bytes 884744 | tf_op jit(solution)/shard_map/ppermute | solution.py:698
  109.8 19.4 %collective-permute-start.20 = (bf16[3,384,128]{2,1,0:T(8,128)(2,1)S(1)}, bf16[3,384,128]{2,1,0:T(8,128)(2,1)S(1)}, u32[]{:S(2)}, u32[]{:S(2)}) collective-permute-start(bf16[3,384,128]{2,1,0:T(8,128)(2,1)S(1)} %collective-permute-done.16.refs_3_), channel_id=1, source_target_pairs={{0,1},{1,0},{2,3},{3,2},{4,5},{5,4},{6,7},{7,6},{8,9},{9,8},{10,11... | collective-permute-start | bytes 884744 | tf_op jit(solution)/shard_map/ppermute | solution.py:698
  203.8 17.9 %collective-permute-start.39 = (bf16[3,4,256,128]{3,2,1,0:T(8,128)(2,1)}, bf16[3,4,256,128]{3,2,1,0:T(8,128)(2,1)S(1)}, u32[]{:S(2)}, u32[]{:S(2)}) collective-permute-start(bf16[3,4,256,128]{3,2,1,0:T(8,128)(2,1)} %get-tuple-element.152), channel_id=1, source_target_pairs={{0,1},{1,0},{2,3},{3,2},{4,5},{5,4},{6,7},{7,6},{8,9},{9,8},{10,11... | collective-permute-start | bytes 2359304 | tf_op jit(solution)/shard_map/ppermute | solution.py:698
  205.4 65.0 %collective-permute-start.27 = (bf16[2,96,4608]{2,1,0:T(8,128)(2,1)S(1)}, bf16[2,96,4608]{2,1,0:T(8,128)(2,1)S(1)}, u32[]{:S(2)}, u32[]{:S(2)}) collective-permute-start(bf16[2,96,4608]{2,1,0:T(8,128)(2,1)S(1)} %copy-done.42), channel_id=1, source_target_pairs={{0,8},{8,0},{16,24},{24,16},{1,9},{9,1},{17,25},{25,17},{2,10},{10... | collective-permute-start | bytes 5308424 | tf_op jit(solution)/shard_map/ppermute | solution.py:698
  224.6 22.4 %collective-permute-start.41 = (bf16[3,384,128]{2,1,0:T(8,128)(2,1)S(1)}, bf16[3,384,128]{2,1,0:T(8,128)(2,1)S(1)}, u32[]{:S(2)}, u32[]{:S(2)}) collective-permute-start(bf16[3,384,128]{2,1,0:T(8,128)(2,1)S(1)} %get-tuple-element.155), channel_id=1, source_target_pairs={{0,4},{1,5},{2,6},{3,7},{4,0},{5,1},{6,2},{7,3},{8,12},{9,13},{10,... | collective-permute-start | bytes 884744 | tf_op jit(solution)/shard_map/ppermute | solution.py:698
  224.6 22.4 %collective-permute-start.42 = (bf16[3,384,128]{2,1,0:T(8,128)(2,1)S(1)}, bf16[3,384,128]{2,1,0:T(8,128)(2,1)S(1)}, u32[]{:S(2)}, u32[]{:S(2)}) collective-permute-start(bf16[3,384,128]{2,1,0:T(8,128)(2,1)S(1)} %get-tuple-element.156), channel_id=1, source_target_pairs={{0,6},{1,7},{2,4},{3,5},{4,2},{5,3},{6,0},{7,1},{8,14},{9,15},{10,... | collective-permute-start | bytes 884744 | tf_op jit(solution)/shard_map/ppermute | solution.py:698
  273.6 47.3 %collective-permute-start.28 = (bf16[96,4608]{1,0:T(8,128)(2,1)S(1)}, bf16[96,4608]{1,0:T(8,128)(2,1)S(1)}, u32[]{:S(2)}, u32[]{:S(2)}) collective-permute-start(bf16[96,4608]{1,0:T(8,128)(2,1)S(1)} %get-tuple-element.126), channel_id=1, source_target_pairs={{0,16},{8,24},{16,0},{24,8},{1,17},{9,25},{17,1},{25,9},{2,18},{10... | collective-permute-start | bytes 2654216 | tf_op jit(solution)/shard_map/ppermute | solution.py:698
  275.5 67.7 %collective-permute-start.44 = (bf16[96,3456]{1,0:T(8,128)(2,1)S(1)}, bf16[96,3456]{1,0:T(8,128)(2,1)S(1)}, u32[]{:S(2)}, u32[]{:S(2)}) collective-permute-start(bf16[96,3456]{1,0:T(8,128)(2,1)S(1)} %get-tuple-element.160), channel_id=1, source_target_pairs={{0,16},{8,24},{16,0},{24,8},{1,17},{9,25},{17,1},{25,9},{2,18},{10... | collective-permute-start | bytes 1990664 | tf_op jit(solution)/shard_map/ppermute | solution.py:698
  277.4 34.2 %collective-permute-start.53 = (f32[8,2304]{1,0:T(8,128)S(1)}, f32[8,2304]{1,0:T(8,128)S(1)}, u32[]{:S(2)}, u32[]{:S(2)}) collective-permute-start(f32[8,2304]{1,0:T(8,128)S(1)} %add.84), channel_id=1, source_target_pairs={{0,16},{8,24},{16,0},{24,8},{1,17},{9,25},{17,1},{25,9},{2,18},{10... | collective-permute-start | bytes 221192 | tf_op jit(solution)/shard_map/ppermute | solution.py:698
  325.0 18.7 %collective-permute-start.31 = (bf16[27,16,128]{2,1,0:T(8,128)(2,1)S(1)}, bf16[27,16,128]{2,1,0:T(8,128)(2,1)S(1)}, u32[]{:S(2)}, u32[]{:S(2)}) collective-permute-start(bf16[27,16,128]{2,1,0:T(8,128)(2,1)S(1)} %get-tuple-element.130), channel_id=1, source_target_pairs={{0,3},{1,2},{2,1},{3,0},{4,7},{5,6},{6,5},{7,4},{8,11},{9,10},{10,... | collective-permute-start | bytes 331784 | tf_op jit(solution)/shard_map/ppermute | solution.py:698
  329.0 16.3 %collective-permute-start.32 = (bf16[27,16,128]{2,1,0:T(8,128)(2,1)S(1)}, bf16[27,16,128]{2,1,0:T(8,128)(2,1)S(1)}, u32[]{:S(2)}, u32[]{:S(2)}) collective-permute-start(bf16[27,16,128]{2,1,0:T(8,128)(2,1)S(1)} %get-tuple-element.131), channel_id=1, source_target_pairs={{0,4},{1,5},{2,6},{3,7},{4,0},{5,1},{6,2},{7,3},{8,12},{9,13},{10,... | collective-permute-start | bytes 331784 | tf_op jit(solution)/shard_map/ppermute | solution.py:698
  333.8 16.0 %collective-permute-start.34 = (bf16[27,16,128]{2,1,0:T(8,128)(2,1)S(1)}, bf16[27,16,128]{2,1,0:T(8,128)(2,1)S(1)}, u32[]{:S(2)}, u32[]{:S(2)}) collective-permute-start(bf16[27,16,128]{2,1,0:T(8,128)(2,1)S(1)} %get-tuple-element.133), channel_id=1, source_target_pairs={{0,6},{1,7},{2,4},{3,5},{4,2},{5,3},{6,0},{7,1},{8,14},{9,15},{10,... | collective-permute-start | bytes 331784 | tf_op jit(solution)/shard_map/ppermute | solution.py:698
  360.0 18.0 %collective-permute-start.63 = (bf16[27,16,128]{2,1,0:T(8,128)(2,1)S(1)}, bf16[27,16,128]{2,1,0:T(8,128)(2,1)S(1)}, u32[]{:S(2)}, u32[]{:S(2)}) collective-permute-start(bf16[27,16,128]{2,1,0:T(8,128)(2,1)S(1)} %get-tuple-element.173.refs_1_), channel_id=1, source_target_pairs={{0,2},{1,3},{2,0},{3,1},{4,6},{5,7},{6,4},{7,5},{8,10},{9,11},{10,... | collective-permute-start | bytes 331784 | tf_op jit(solution)/shard_map/ppermute | solution.py:698
  363.6 17.8 %collective-permute-start.64 = (bf16[27,16,128]{2,1,0:T(8,128)(2,1)S(1)}, bf16[27,16,128]{2,1,0:T(8,128)(2,1)S(1)}, u32[]{:S(2)}, u32[]{:S(2)}) collective-permute-start(bf16[27,16,128]{2,1,0:T(8,128)(2,1)S(1)} %get-tuple-element.173.refs_1_), channel_id=1, source_target_pairs={{0,3},{1,2},{2,1},{3,0},{4,7},{5,6},{6,5},{7,4},{8,11},{9,10},{10,... | collective-permute-start | bytes 331784 | tf_op jit(solution)/shard_map/ppermute | solution.py:698
  388.3 16.4 %collective-permute-start.71 = (bf16[21,16,128]{2,1,0:T(8,128)(2,1)S(1)}, bf16[21,16,128]{2,1,0:T(8,128)(2,1)S(1)}, u32[]{:S(2)}, u32[]{:S(2)}) collective-permute-start(bf16[21,16,128]{2,1,0:T(8,128)(2,1)S(1)} %get-tuple-element.174.refs_9_), channel_id=1, source_target_pairs={{0,3},{1,2},{2,1},{3,0},{4,7},{5,6},{6,5},{7,4},{8,11},{9,10},{10,... | collective-permute-start | bytes 258056 | tf_op jit(solution)/shard_map/ppermute | solution.py:698
  (96 other events, 1397.9 us)
